TPU v7x, 256 devices: a whole 4x4x8 slice. The times are simulated.
256 devices in a mesh: ctx: 32 (over z, y_lo, core), resp: 8 (over x, y_hi).
Axes of the slice: x: 4, y: 4 (y_hi: 2, y_lo: 2; y = y_hi * 2 + y_lo), z: 8, core: 2. Of those that a mesh axis runs over, the one named last changes fastest.
Arguments:
- prompt_q: bfloat16 [4096, 8192], P('ctx', 'resp'), may hold values from -4.5 to 4.5
- prompt_k: bfloat16 [4096, 1024], P('ctx', 'resp'), may hold values from -4.5 to 4.5
- prompt_v: bfloat16 [4096, 1024], P('ctx', 'resp'), may hold values from -6 to 6
- prompt_out: bfloat16 [4096, 8192], P('ctx', 'resp'), may hold values from -3 to 3
- prompt_dout: bfloat16 [4096, 8192], P('ctx', 'resp'), may hold values from -1.5 to 1.5
- resp_q: bfloat16 [4096, 8192], P(('ctx', 'resp')), may hold values from -4.5 to 4.5
- resp_k: bfloat16 [4096, 1024], P(('ctx', 'resp')), may hold values from -6 to 6
- resp_v: bfloat16 [4096, 1024], P(('ctx', 'resp')), may hold values from -6 to 6
- resp_out: bfloat16 [4096, 8192], P(('ctx', 'resp')), may hold values from -3 to 3
- resp_dout: bfloat16 [4096, 8192], P(('ctx', 'resp')), may hold values from -1.5 to 1.5
- lengths: int32 [16], replicated, may hold values from 1 to 128, as said below
- resp_row: int32 [16], replicated, may hold values from 0 to 31
- block_index: int32 [32], replicated, may hold values from 0 to 31, each once
Outputs:
- prompt_dq: bfloat16 [4096, 8192], P('ctx', 'resp')
- prompt_dk: bfloat16 [4096, 1024], P('ctx', 'resp')
- prompt_dv: bfloat16 [4096, 1024], P('ctx', 'resp')
- resp_dq: bfloat16 [4096, 8192], P(('ctx', 'resp'))
- resp_dk: bfloat16 [4096, 1024], P(('ctx', 'resp'))
- resp_dv: bfloat16 [4096, 1024], P(('ctx', 'resp'))
Inputs may be any that keep to these rules, and one draw needn't show every extreme that they name: `lengths`: the responses named to one index of ctx lie in its 128 slots one after another in order of their number from its first slot, and together fill exactly 128 slots; an index named by no response holds none.
All inputs are finite; a program needn't handle non-finite values.
Results may differ from a plain program's by a relative error of at most 0.005.
Values may be sent and summed in bfloat16 or wider, within the bound.
A program may use at most 64 MiB of HBM per device.

v0:
```python
import math

import jax
import jax.numpy as jnp
from jax import lax
from jax.sharding import PartitionSpec as P

HEAD_DIM = 128
Q_HEADS = 64
KV_HEADS = 8


START_PEAK = -1e30


def slot_layout(lengths, resp_row, row_here, row_tok, prompt_len):
    number = jnp.arange(lengths.shape[0], dtype=jnp.int32)
    same_row = resp_row[:, None] == resp_row[None, :]
    earlier = same_row & (number[None, :] < number[:, None])
    first_slot = jnp.sum(jnp.where(earlier, lengths[None, :], 0), axis=1)
    slot_ids = jnp.arange(row_tok, dtype=jnp.int32)
    member = (
        (resp_row[:, None] == row_here)
        & (slot_ids[None, :] >= first_slot[:, None])
        & (slot_ids[None, :] < first_slot[:, None] + lengths[:, None])
    )
    slot_owner = jnp.where(
        jnp.any(member, axis=0), jnp.sum(jnp.where(member, number[:, None], 0), axis=0), -2
    )
    slot_place = prompt_len + slot_ids - jnp.sum(jnp.where(member, first_slot[:, None], 0), axis=0)
    return (slot_owner, slot_place)


def masked_scores(queries, key_rows, visible):
    scores = jnp.einsum("qhgd,khd->hgqk", queries, key_rows, preferred_element_type=jnp.float32)
    scores = scores * HEAD_DIM ** (-0.5)
    return jnp.where(visible[None, None], scores, -jnp.inf)


def stats_step(stat_pair, queries, key_rows, visible):
    peak_score, total_exp = stat_pair
    scores = masked_scores(queries, key_rows, visible)
    new_peak = jnp.maximum(peak_score, jnp.max(scores, axis=3))
    total_exp = total_exp * jnp.exp(peak_score - new_peak) + jnp.sum(
        jnp.exp(scores - new_peak[..., None]), axis=3
    )
    return (new_peak, total_exp)


def finish_stats(stat_pair):
    peak_score, total_exp = stat_pair
    filled = total_exp > 0.0
    return jnp.where(filled, peak_score + jnp.log(jnp.where(filled, total_exp, 1.0)), 0.0)


def grad_step(queries, cotangent, log_total, delta, key_rows, value_rows, visible):
    scores = masked_scores(queries, key_rows, visible)
    probs = jnp.exp(scores - log_total[..., None])
    prob_half = probs.astype(jnp.bfloat16)
    dprob = jnp.einsum("qhgd,khd->hgqk", cotangent, value_rows, preferred_element_type=jnp.float32)
    dscore = (probs * (dprob - delta[..., None])).astype(jnp.bfloat16)
    score_scale = HEAD_DIM ** (-0.5)
    query_grad = score_scale * jnp.einsum(
        "hgqk,khd->qhgd", dscore, key_rows, preferred_element_type=jnp.float32
    )
    key_grad = score_scale * jnp.einsum(
        "hgqk,qhgd->khd", dscore, queries, preferred_element_type=jnp.float32
    )
    value_grad = jnp.einsum(
        "hgqk,qhgd->khd", prob_half, cotangent, preferred_element_type=jnp.float32
    )
    return (query_grad, key_grad, value_grad)


def body(
    prompt_q,
    prompt_k,
    prompt_v,
    prompt_out,
    prompt_dout,
    resp_q,
    resp_k,
    resp_v,
    resp_out,
    resp_dout,
    lengths,
    resp_row,
    block_index,
):
    block_len = prompt_q.shape[0]
    kv_dev = prompt_k.shape[1] // HEAD_DIM
    group_size = Q_HEADS // KV_HEADS
    ctx_count = lax.axis_size("ctx")
    ctx_here = lax.axis_index("ctx")
    prompt_len = block_len * ctx_count
    my_block = block_index[ctx_here]
    prompt_place = my_block * block_len + jnp.arange(block_len, dtype=jnp.int32)
    latest_place = my_block * block_len + block_len - 1

    def as_queries(row_data):
        return row_data.reshape(row_data.shape[0], kv_dev, group_size, HEAD_DIM)

    def as_keys(row_data):
        return row_data.reshape(row_data.shape[0], kv_dev, HEAD_DIM)

    def row_delta(outputs, cotangent):
        summed = jnp.sum(outputs.astype(jnp.float32) * cotangent.astype(jnp.float32), axis=3)
        return jnp.transpose(summed, (1, 2, 0))

    def fresh_stats(row_count):
        return (
            jnp.full((kv_dev, group_size, row_count), START_PEAK, dtype=jnp.float32),
            jnp.zeros((kv_dev, group_size, row_count), dtype=jnp.float32),
        )

    def key_places(first_row, row_count):
        row_ids = first_row + jnp.arange(row_count, dtype=jnp.int32)
        return block_index[row_ids // block_len] * block_len + row_ids % block_len

    row_query, row_output, row_cot, row_key, row_value = (
        lax.all_to_all(resp_q, "resp", split_axis=1, concat_axis=0, tiled=True),
        lax.all_to_all(resp_out, "resp", split_axis=1, concat_axis=0, tiled=True),
        lax.all_to_all(resp_dout, "resp", split_axis=1, concat_axis=0, tiled=True),
        lax.all_to_all(resp_k, "resp", split_axis=1, concat_axis=0, tiled=True),
        lax.all_to_all(resp_v, "resp", split_axis=1, concat_axis=0, tiled=True),
    )
    row_tok = row_query.shape[0]
    slot_owner, slot_place = slot_layout(lengths, resp_row, ctx_here, row_tok, prompt_len)
    live_slot = slot_owner >= 0
    row_busy = jnp.any(live_slot)
    own_visible = (
        (slot_owner[None, :] == slot_owner[:, None])
        & live_slot[:, None]
        & (slot_place[None, :] <= slot_place[:, None])
    )
    prompt_query = as_queries(prompt_q)
    prompt_cot = as_queries(prompt_dout)
    prompt_delta = row_delta(as_queries(prompt_out), prompt_cot)
    slot_query = as_queries(row_query)
    slot_cot = as_queries(row_cot)
    slot_delta = row_delta(as_queries(row_output), slot_cot)
    slot_keys = as_keys(row_key)
    slot_values = as_keys(row_value)

    def stats_block(stat_sets, key_rows, key_place):
        prompt_stats, slot_stats = stat_sets
        prompt_stats = lax.cond(
            jnp.min(key_place) <= latest_place,
            lambda: stats_step(
                prompt_stats, prompt_query, key_rows, key_place[None, :] <= prompt_place[:, None]
            ),
            lambda: prompt_stats,
        )
        slot_stats = lax.cond(
            row_busy,
            lambda: stats_step(
                slot_stats,
                slot_query,
                key_rows,
                jnp.broadcast_to(live_slot[:, None], (row_tok, key_rows.shape[0])),
            ),
            lambda: slot_stats,
        )
        return (prompt_stats, slot_stats)

    slot_start = stats_step(fresh_stats(row_tok), slot_query, slot_keys, own_visible)
    stat_start = (fresh_stats(block_len), slot_start)
    carried = stat_start
    pieces = lax.all_gather(as_keys(prompt_k), "ctx", axis=0, tiled=True)
    row_count = pieces.shape[0]
    sub_size = math.gcd(row_count, 512)
    sub_parts = pieces.reshape(row_count // sub_size, sub_size, kv_dev, HEAD_DIM)
    sub_first = sub_size * jnp.arange(row_count // sub_size, dtype=jnp.int32)

    def stats_visit(inner_stats, sub_items):
        key_rows, sub_row = sub_items
        return (stats_block(inner_stats, key_rows, key_places(sub_row, sub_size)), None)

    carried, unused = lax.scan(stats_visit, carried, (sub_parts, sub_first))
    prompt_stats, slot_stats = carried
    prompt_lse = finish_stats(prompt_stats)
    slot_lse = finish_stats(slot_stats)

    def grads_block(query_sums, key_rows, value_rows, key_place):
        prompt_sum, slot_sum = query_sums
        zero_keys = jnp.zeros(key_rows.shape, dtype=jnp.float32)

        def prompt_part():
            return grad_step(
                prompt_query,
                prompt_cot,
                prompt_lse,
                prompt_delta,
                key_rows,
                value_rows,
                key_place[None, :] <= prompt_place[:, None],
            )

        def prompt_none():
            return (jnp.zeros(prompt_query.shape, dtype=jnp.float32), zero_keys, zero_keys)

        def slot_part():
            return grad_step(
                slot_query,
                slot_cot,
                slot_lse,
                slot_delta,
                key_rows,
                value_rows,
                jnp.broadcast_to(live_slot[:, None], (row_tok, key_rows.shape[0])),
            )

        def slot_none():
            return (jnp.zeros(slot_query.shape, dtype=jnp.float32), zero_keys, zero_keys)

        prompt_dq_part, prompt_dk_part, prompt_dv_part = lax.cond(
            jnp.min(key_place) <= latest_place, prompt_part, prompt_none
        )
        slot_dq_part, slot_dk_part, slot_dv_part = lax.cond(row_busy, slot_part, slot_none)
        return (
            (prompt_sum + prompt_dq_part, slot_sum + slot_dq_part),
            prompt_dk_part + slot_dk_part,
            prompt_dv_part + slot_dv_part,
        )

    query_start = (
        jnp.zeros(prompt_query.shape, dtype=jnp.float32),
        jnp.zeros(slot_query.shape, dtype=jnp.float32),
    )
    query_sums = query_start
    key_pieces = lax.all_gather(as_keys(prompt_k), "ctx", axis=0, tiled=True)
    value_pieces = lax.all_gather(as_keys(prompt_v), "ctx", axis=0, tiled=True)
    row_count = key_pieces.shape[0]
    grads_sub_size = math.gcd(row_count, 512)
    sub_keys = key_pieces.reshape(row_count // grads_sub_size, grads_sub_size, kv_dev, HEAD_DIM)
    sub_values = value_pieces.reshape(row_count // grads_sub_size, grads_sub_size, kv_dev, HEAD_DIM)
    sub_first = grads_sub_size * jnp.arange(row_count // grads_sub_size, dtype=jnp.int32)

    def grads_visit(inner_sums, sub_items):
        key_rows, value_rows, sub_row = sub_items
        inner_sums, key_part, value_part = grads_block(
            inner_sums, key_rows, value_rows, key_places(sub_row, grads_sub_size)
        )
        return (inner_sums, (key_part, value_part))

    query_sums, (key_parts, value_parts) = lax.scan(
        grads_visit, query_sums, (sub_keys, sub_values, sub_first)
    )
    key_grad_all = key_parts.reshape(row_count, kv_dev, HEAD_DIM)
    value_grad_all = value_parts.reshape(row_count, kv_dev, HEAD_DIM)
    query_sums, key_grad_all, value_grad_all = (query_sums, key_grad_all, value_grad_all)
    prompt_key_grad, prompt_value_grad = (
        lax.psum_scatter(key_grad_all, "ctx", scatter_dimension=0, tiled=True),
        lax.psum_scatter(value_grad_all, "ctx", scatter_dimension=0, tiled=True),
    )
    own_dq, own_dk, own_dv = grad_step(
        slot_query, slot_cot, slot_lse, slot_delta, slot_keys, slot_values, own_visible
    )
    prompt_sum, slot_sum = query_sums
    slot_dq_rows = (slot_sum + own_dq).reshape(row_tok, -1).astype(jnp.bfloat16)
    slot_dk_rows = own_dk.reshape(row_tok, -1).astype(jnp.bfloat16)
    slot_dv_rows = own_dv.reshape(row_tok, -1).astype(jnp.bfloat16)
    resp_dq, resp_dk, resp_dv = (
        lax.all_to_all(slot_dq_rows, "resp", split_axis=0, concat_axis=1, tiled=True),
        lax.all_to_all(slot_dk_rows, "resp", split_axis=0, concat_axis=1, tiled=True),
        lax.all_to_all(slot_dv_rows, "resp", split_axis=0, concat_axis=1, tiled=True),
    )
    prompt_dq = prompt_sum.reshape(block_len, -1).astype(jnp.bfloat16)
    prompt_dk = prompt_key_grad.reshape(block_len, -1).astype(jnp.bfloat16)
    prompt_dv = prompt_value_grad.reshape(block_len, -1).astype(jnp.bfloat16)
    return (prompt_dq, prompt_dk, prompt_dv, resp_dq, resp_dk, resp_dv)


def solution(mesh):
    return jax.shard_map(
        body,
        mesh=mesh,
        in_specs=(
            P("ctx", "resp"),
            P("ctx", "resp"),
            P("ctx", "resp"),
            P("ctx", "resp"),
            P("ctx", "resp"),
            P(("ctx", "resp"), None),
            P(("ctx", "resp"), None),
            P(("ctx", "resp"), None),
            P(("ctx", "resp"), None),
            P(("ctx", "resp"), None),
            P(),
            P(),
            P(),
        ),
        out_specs=(
            P("ctx", "resp"),
            P("ctx", "resp"),
            P("ctx", "resp"),
            P(("ctx", "resp"), None),
            P(("ctx", "resp"), None),
            P(("ctx", "resp"), None),
        ),
        check_vma=False,
    )
```

profile of v0, /device:TPU:1, one launch (start us, length us, event | category | flops | bytes accessed | tf_op | source)
XLA Modules:
  0.0 1065.3 jit_solution(9091015071309755704)
XLA Ops:
  9.6 7.5 all-to-all-start.3
  24.5 6.1 all-to-all-start.2
  31.6 6.4 all-to-all-done.2
  52.5 6.0 all-to-all-done
  59.7 18.1 %all-gather.5.cloned.1.call-done = bf16[4096,128]{1,0:T(8,128)(2,1)} async-done(((bf16[128,128]{1,0:T(8,128)(2,1)}), bf16[4096,128]{1,0:T(8,128)(2,1)}) %all-gather.5.cloned.1.call-update) | async-done | bytes 1048592 | tf_op jit(solution)/shard_map/all_gather | solution.py:231
  77.7 295.6 %while.38 = (s32[]{:T(128)}, f32[1,8,128]{2,1,0:T(8,128)S(1)}, f32[1,8,128]{2,1,0:T(8,128)S(1)}, f32[1,8,128]{2,1,0:T(8,128)S(1)}, f32[1,8,128]{2,1,0:T(8,128)S(...) while((s32[]{:T(128)}, f32[1,8,128]{2,1,0:T(8,128)S(1)}, ...), condition=%wide.region_17.18_spmd.clone, body=%wide.region_7.17_spmd.clone.sunk | while | flops 276020864 | bytes 9777196 | solution.py:179
  89.3 5.2 compare_select_fusion.26
  95.1 16.8 %fusion.111 = (s32[]{:T(128)}, s32[512]{0:T(512)S(1)}) fusion(s32[]{:T(128)} %bitcast.520, pred[512]{0:T(512)(128)(4,1)S(1)} %get-tuple-element.1291, pred[512]{0:T(512)(128)(4,1)S(1)} %get-tuple-element.1292, pred[512]{0:T(512)(128)(4,1)S(1)} %get-tuple-element.1293, pred[512]{0:T(512)(128)(4,1)S(1)} %get-tuple-element.1294, ...), kind=kLoop, calls=%fused_computation.226.clone.1 | loop fusion | flops 20479 | bytes 17004 | tf_op jit(solution)/shard_map/while/body/eval_jaxpr/reduce_min | solution.py:148
  126.2 5.2 compare_select_fusion.26
  132.1 16.8 %fusion.111 = (s32[]{:T(128)}, s32[512]{0:T(512)S(1)}) fusion(s32[]{:T(128)} %bitcast.520, pred[512]{0:T(512)(128)(4,1)S(1)} %get-tuple-element.1291, pred[512]{0:T(512)(128)(4,1)S(1)} %get-tuple-element.1292, pred[512]{0:T(512)(128)(4,1)S(1)} %get-tuple-element.1293, pred[512]{0:T(512)(128)(4,1)S(1)} %get-tuple-element.1294, ...), kind=kLoop, calls=%fused_computation.226.clone.1 | loop fusion | flops 20479 | bytes 17004 | tf_op jit(solution)/shard_map/while/body/eval_jaxpr/reduce_min | solution.py:148
  163.2 5.2 compare_select_fusion.26
  169.0 16.8 %fusion.111 = (s32[]{:T(128)}, s32[512]{0:T(512)S(1)}) fusion(s32[]{:T(128)} %bitcast.520, pred[512]{0:T(512)(128)(4,1)S(1)} %get-tuple-element.1291, pred[512]{0:T(512)(128)(4,1)S(1)} %get-tuple-element.1292, pred[512]{0:T(512)(128)(4,1)S(1)} %get-tuple-element.1293, pred[512]{0:T(512)(128)(4,1)S(1)} %get-tuple-element.1294, ...), kind=kLoop, calls=%fused_computation.226.clone.1 | loop fusion | flops 20479 | bytes 17004 | tf_op jit(solution)/shard_map/while/body/eval_jaxpr/reduce_min | solution.py:148
  206.0 16.8 %fusion.111 = (s32[]{:T(128)}, s32[512]{0:T(512)S(1)}) fusion(s32[]{:T(128)} %bitcast.520, pred[512]{0:T(512)(128)(4,1)S(1)} %get-tuple-element.1291, pred[512]{0:T(512)(128)(4,1)S(1)} %get-tuple-element.1292, pred[512]{0:T(512)(128)(4,1)S(1)} %get-tuple-element.1293, pred[512]{0:T(512)(128)(4,1)S(1)} %get-tuple-element.1294, ...), kind=kLoop, calls=%fused_computation.226.clone.1 | loop fusion | flops 20479 | bytes 17004 | tf_op jit(solution)/shard_map/while/body/eval_jaxpr/reduce_min | solution.py:148
  242.9 16.8 %fusion.111 = (s32[]{:T(128)}, s32[512]{0:T(512)S(1)}) fusion(s32[]{:T(128)} %bitcast.520, pred[512]{0:T(512)(128)(4,1)S(1)} %get-tuple-element.1291, pred[512]{0:T(512)(128)(4,1)S(1)} %get-tuple-element.1292, pred[512]{0:T(512)(128)(4,1)S(1)} %get-tuple-element.1293, pred[512]{0:T(512)(128)(4,1)S(1)} %get-tuple-element.1294, ...), kind=kLoop, calls=%fused_computation.226.clone.1 | loop fusion | flops 20479 | bytes 17004 | tf_op jit(solution)/shard_map/while/body/eval_jaxpr/reduce_min | solution.py:148
  279.9 16.8 %fusion.111 = (s32[]{:T(128)}, s32[512]{0:T(512)S(1)}) fusion(s32[]{:T(128)} %bitcast.520, pred[512]{0:T(512)(128)(4,1)S(1)} %get-tuple-element.1291, pred[512]{0:T(512)(128)(4,1)S(1)} %get-tuple-element.1292, pred[512]{0:T(512)(128)(4,1)S(1)} %get-tuple-element.1293, pred[512]{0:T(512)(128)(4,1)S(1)} %get-tuple-element.1294, ...), kind=kLoop, calls=%fused_computation.226.clone.1 | loop fusion | flops 20479 | bytes 17004 | tf_op jit(solution)/shard_map/while/body/eval_jaxpr/reduce_min | solution.py:148
  316.8 16.8 %fusion.111 = (s32[]{:T(128)}, s32[512]{0:T(512)S(1)}) fusion(s32[]{:T(128)} %bitcast.520, pred[512]{0:T(512)(128)(4,1)S(1)} %get-tuple-element.1291, pred[512]{0:T(512)(128)(4,1)S(1)} %get-tuple-element.1292, pred[512]{0:T(512)(128)(4,1)S(1)} %get-tuple-element.1293, pred[512]{0:T(512)(128)(4,1)S(1)} %get-tuple-element.1294, ...), kind=kLoop, calls=%fused_computation.226.clone.1 | loop fusion | flops 20479 | bytes 17004 | tf_op jit(solution)/shard_map/while/body/eval_jaxpr/reduce_min | solution.py:148
  353.8 16.8 %fusion.111 = (s32[]{:T(128)}, s32[512]{0:T(512)S(1)}) fusion(s32[]{:T(128)} %bitcast.520, pred[512]{0:T(512)(128)(4,1)S(1)} %get-tuple-element.1291, pred[512]{0:T(512)(128)(4,1)S(1)} %get-tuple-element.1292, pred[512]{0:T(512)(128)(4,1)S(1)} %get-tuple-element.1293, pred[512]{0:T(512)(128)(4,1)S(1)} %get-tuple-element.1294, ...), kind=kLoop, calls=%fused_computation.226.clone.1 | loop fusion | flops 20479 | bytes 17004 | tf_op jit(solution)/shard_map/while/body/eval_jaxpr/reduce_min | solution.py:148
  374.6 418.0 %while.39 = (s32[]{:T(128)}, f32[128,1,8,128]{3,0,2,1:T(8,128)}, f32[128,1,8,128]{3,0,2,1:T(8,128)}, f32[8,512,1,128]{3,1,2,0:T(8,128)}, f32[8,512,1,128]{3,1,2,...) while((s32[]{:T(128)}, f32[128,1,8,128]{3,0,2,1:T(8,128)}, ...), condition=%wide.region_26.27_spmd.clone, body=%wide.region_20.26_spmd.clone.sunk | while | flops 1350923904 | bytes 29282348 | solution.py:246
  400.9 16.9 %fusion.114 = (s32[]{:T(128)}, s32[512]{0:T(512)S(1)}) fusion(s32[]{:T(128)} %bitcast.557, pred[512]{0:T(512)(128)(4,1)S(1)} %compare_reduce_fusion.101, pred[512]{0:T(512)(128)(4,1)S(1)} %compare_reduce_fusion.102, pred[512]{0:T(512)(128)(4,1)S(1)} %compare_reduce_fusion.103, pred[512]{0:T(512)(128)(4,1)S(1)} %compare_reduce_fusion.104, ...), kind=kLoop, calls=%fused_computation.227.clone.1 | loop fusion | flops 20479 | bytes 17004 | tf_op jit(solution)/shard_map/while/body/eval_jaxpr/reduce_min | solution.py:217
  452.2 16.9 %fusion.114 = (s32[]{:T(128)}, s32[512]{0:T(512)S(1)}) fusion(s32[]{:T(128)} %bitcast.557, pred[512]{0:T(512)(128)(4,1)S(1)} %compare_reduce_fusion.101, pred[512]{0:T(512)(128)(4,1)S(1)} %compare_reduce_fusion.102, pred[512]{0:T(512)(128)(4,1)S(1)} %compare_reduce_fusion.103, pred[512]{0:T(512)(128)(4,1)S(1)} %compare_reduce_fusion.104, ...), kind=kLoop, calls=%fused_computation.227.clone.1 | loop fusion | flops 20479 | bytes 17004 | tf_op jit(solution)/shard_map/while/body/eval_jaxpr/reduce_min | solution.py:217
  504.6 16.9 %fusion.114 = (s32[]{:T(128)}, s32[512]{0:T(512)S(1)}) fusion(s32[]{:T(128)} %bitcast.557, pred[512]{0:T(512)(128)(4,1)S(1)} %compare_reduce_fusion.101, pred[512]{0:T(512)(128)(4,1)S(1)} %compare_reduce_fusion.102, pred[512]{0:T(512)(128)(4,1)S(1)} %compare_reduce_fusion.103, pred[512]{0:T(512)(128)(4,1)S(1)} %compare_reduce_fusion.104, ...), kind=kLoop, calls=%fused_computation.227.clone.1 | loop fusion | flops 20479 | bytes 17004 | tf_op jit(solution)/shard_map/while/body/eval_jaxpr/reduce_min | solution.py:217
  557.0 16.9 %fusion.114 = (s32[]{:T(128)}, s32[512]{0:T(512)S(1)}) fusion(s32[]{:T(128)} %bitcast.557, pred[512]{0:T(512)(128)(4,1)S(1)} %compare_reduce_fusion.101, pred[512]{0:T(512)(128)(4,1)S(1)} %compare_reduce_fusion.102, pred[512]{0:T(512)(128)(4,1)S(1)} %compare_reduce_fusion.103, pred[512]{0:T(512)(128)(4,1)S(1)} %compare_reduce_fusion.104, ...), kind=kLoop, calls=%fused_computation.227.clone.1 | loop fusion | flops 20479 | bytes 17004 | tf_op jit(solution)/shard_map/while/body/eval_jaxpr/reduce_min | solution.py:217
  609.4 16.9 %fusion.114 = (s32[]{:T(128)}, s32[512]{0:T(512)S(1)}) fusion(s32[]{:T(128)} %bitcast.557, pred[512]{0:T(512)(128)(4,1)S(1)} %compare_reduce_fusion.101, pred[512]{0:T(512)(128)(4,1)S(1)} %compare_reduce_fusion.102, pred[512]{0:T(512)(128)(4,1)S(1)} %compare_reduce_fusion.103, pred[512]{0:T(512)(128)(4,1)S(1)} %compare_reduce_fusion.104, ...), kind=kLoop, calls=%fused_computation.227.clone.1 | loop fusion | flops 20479 | bytes 17004 | tf_op jit(solution)/shard_map/while/body/eval_jaxpr/reduce_min | solution.py:217
  661.8 16.9 %fusion.114 = (s32[]{:T(128)}, s32[512]{0:T(512)S(1)}) fusion(s32[]{:T(128)} %bitcast.557, pred[512]{0:T(512)(128)(4,1)S(1)} %compare_reduce_fusion.101, pred[512]{0:T(512)(128)(4,1)S(1)} %compare_reduce_fusion.102, pred[512]{0:T(512)(128)(4,1)S(1)} %compare_reduce_fusion.103, pred[512]{0:T(512)(128)(4,1)S(1)} %compare_reduce_fusion.104, ...), kind=kLoop, calls=%fused_computation.227.clone.1 | loop fusion | flops 20479 | bytes 17004 | tf_op jit(solution)/shard_map/while/body/eval_jaxpr/reduce_min | solution.py:217
  714.2 16.9 %fusion.114 = (s32[]{:T(128)}, s32[512]{0:T(512)S(1)}) fusion(s32[]{:T(128)} %bitcast.557, pred[512]{0:T(512)(128)(4,1)S(1)} %compare_reduce_fusion.101, pred[512]{0:T(512)(128)(4,1)S(1)} %compare_reduce_fusion.102, pred[512]{0:T(512)(128)(4,1)S(1)} %compare_reduce_fusion.103, pred[512]{0:T(512)(128)(4,1)S(1)} %compare_reduce_fusion.104, ...), kind=kLoop, calls=%fused_computation.227.clone.1 | loop fusion | flops 20479 | bytes 17004 | tf_op jit(solution)/shard_map/while/body/eval_jaxpr/reduce_min | solution.py:217
  766.5 16.9 %fusion.114 = (s32[]{:T(128)}, s32[512]{0:T(512)S(1)}) fusion(s32[]{:T(128)} %bitcast.557, pred[512]{0:T(512)(128)(4,1)S(1)} %compare_reduce_fusion.101, pred[512]{0:T(512)(128)(4,1)S(1)} %compare_reduce_fusion.102, pred[512]{0:T(512)(128)(4,1)S(1)} %compare_reduce_fusion.103, pred[512]{0:T(512)(128)(4,1)S(1)} %compare_reduce_fusion.104, ...), kind=kLoop, calls=%fused_computation.227.clone.1 | loop fusion | flops 20479 | bytes 17004 | tf_op jit(solution)/shard_map/while/body/eval_jaxpr/reduce_min | solution.py:217
  793.9 6.2 all-to-all-start.4
  801.0 5.6 all-to-all-done.4
  811.1 5.4 all-to-all-done.7
  831.0 6.0 all-to-all-done.5
  837.7 100.2 %reduce-scatter.5.cloned.1.call-done = f32[128,1,128]{2,0,1:T(8,128)} async-done(((f32[4096,1,128]{2,0,1:T(8,128)}), f32[128,1,128]{2,0,1:T(8,128)}) %reduce-scatter.5.cloned.1.call-update) | async-done | bytes 65552 | tf_op jit(solution)/shard_map/reduce_scatter | solution.py:254
  939.4 117.9 %reduce-scatter.3.cloned.1.call-done = f32[128,1,128]{2,0,1:T(8,128)} async-done(((f32[4096,1,128]{2,0,1:T(8,128)}), f32[128,1,128]{2,0,1:T(8,128)}) %reduce-scatter.3.cloned.1.call-update) | async-done | bytes 65552 | tf_op jit(solution)/shard_map/reduce_scatter | solution.py:253
  (693 shorter events, 492.7 us)
Async XLA Ops:
  7.2 36.6 %copy-start = (bf16[16,1024]{1,0:T(8,128)(2,1)S(1)}, bf16[16,1024]{1,0:T(8,128)(2,1)}, u32[]{:S(2)}) copy-start(bf16[16,1024]{1,0:T(8,128)(2,1)} %param.31) | copy-start | bytes 98308
  7.2 16.1 %copy-start.10 = (bf16[16,8192]{1,0:T(8,128)(2,1)S(1)}, bf16[16,8192]{1,0:T(8,128)(2,1)}, u32[]{:S(2)}) copy-start(bf16[16,8192]{1,0:T(8,128)(2,1)} %param.34) | copy-start | bytes 786436
  7.2 23.5 %copy-start.11 = (bf16[16,8192]{1,0:T(8,128)(2,1)S(1)}, bf16[16,8192]{1,0:T(8,128)(2,1)}, u32[]{:S(2)}) copy-start(bf16[16,8192]{1,0:T(8,128)(2,1)} %param.30) | copy-start | bytes 786436
  7.2 70.5 %all-gather.5.cloned.1.call-start = ((), (), s32[]{:S(2)}) async-start(), calls=%async_computation.12 | async-start | bytes 1081344 | tf_op jit(solution)/shard_map/all_gather | solution.py:231
  9.6 14.9 %all-to-all-start.3 = ((bf16[16,8,1024]{2,0,1:T(8,128)(2,1)}), bf16[16,8,1024]{2,0,1:T(8,128)(2,1)S(1)}, u32[]{:S(2)}, u32[]{:S(2)}) async-start(bf16[16,8,1024]{2,0,1:T(8,128)(2,1)} %bitcast.444), calls=%async_computation.3 | async-start | bytes 524288 | tf_op jit(solution)/shard_map/all_to_all | solution.py:122
  17.1 357.5 %all-gather.7.cloned.1.call-start = ((), (), s32[]{:S(2)}) async-start(), calls=%async_computation.13 | async-start | bytes 1081344 | tf_op jit(solution)/shard_map/all_gather | solution.py:232
  21.0 21.1 %copy-start.12 = (bf16[128,1024]{1,0:T(8,128)(2,1)S(1)}, bf16[128,1024]{1,0:T(8,128)(2,1)}, u32[]{:S(2)}) copy-start(bf16[128,1024]{1,0:T(8,128)(2,1)} %param.25) | copy-start | bytes 786436
  23.3 19.2 %copy-start.1 = (s32[32]{0:T(128)S(1)}, s32[32]{0:T(128)}, u32[]{:S(2)}) copy-start(s32[32]{0:T(128)} %param.37) | copy-start | bytes 388
  24.5 13.4 %all-to-all-start.2 = ((bf16[16,8,1024]{2,0,1:T(8,128)(2,1)}), bf16[16,8,1024]{2,0,1:T(8,128)(2,1)S(1)}, u32[]{:S(2)}, u32[]{:S(2)}) async-start(bf16[16,8,1024]{2,0,1:T(8,128)(2,1)} %bitcast.445), calls=%async_computation.2 | async-start | bytes 524288 | tf_op jit(solution)/shard_map/all_to_all | solution.py:123
  37.9 10.7 %all-to-all-start.1 = ((bf16[16,8,1024]{2,0,1:T(8,128)(2,1)}), bf16[16,8,1024]{2,0,1:T(8,128)(2,1)S(1)}, u32[]{:S(2)}, u32[]{:S(2)}) async-start(bf16[16,8,1024]{2,0,1:T(8,128)(2,1)} %bitcast.446), calls=%async_computation.1 | async-start | bytes 524288 | tf_op jit(solution)/shard_map/all_to_all | solution.py:121
  44.6 7.8 copy-start.6
  48.6 9.8 all-to-all-start
  52.0 886.0 %reduce-scatter.5.cloned.1.call-start = ((), (), s32[]{:S(2)}) async-start(), calls=%async_computation.11 | async-start | bytes 2162688 | tf_op jit(solution)/shard_map/reduce_scatter | solution.py:254
  52.4 25.4 %copy-start.8 = (bf16[16,8,8,128]{3,2,1,0:T(8,128)(2,1)}, bf16[16,8,8,128]{3,2,1,0:T(8,128)(2,1)S(1)}, u32[]{:S(2)}) copy-start(bf16[16,8,8,128]{3,2,1,0:T(8,128)(2,1)S(1)} %copy.145) | copy-start | bytes 786436
  58.7 0.8 copy-start.4
  792.6 0.8 copy-start.14
  792.6 7.6 copy-start.5
  792.6 7.6 copy-start.7
  792.6 7.6 copy-start.13
  792.6 264.7 %reduce-scatter.3.cloned.1.call-start = ((), (), s32[]{:S(2)}) async-start(), calls=%async_computation.10 | async-start | bytes 2162688 | tf_op jit(solution)/shard_map/reduce_scatter | solution.py:253
  792.6 17.6 %copy-start.9 = (bf16[16,8,8,128]{3,2,1,0:T(8,128)(2,1)S(1)}, bf16[16,8,8,128]{3,2,1,0:T(8,128)(2,1)}, u32[]{:S(2)}) copy-start(bf16[16,8,8,128]{3,2,1,0:T(8,128)(2,1)} %copy-done.8) | copy-start | bytes 786436
  792.7 27.2 %copy-start.3 = (f32[128,1,8,128]{3,0,2,1:T(8,128)S(1)}, f32[128,1,8,128]{3,0,2,1:T(8,128)}, u32[]{:S(2)}) copy-start(f32[128,1,8,128]{3,0,2,1:T(8,128)} %get-tuple-element.559) | copy-start | bytes 1572868
  793.9 12.7 %all-to-all-start.4 = ((bf16[16,8,128]{2,0,1:T(8,128)(2,1)}), bf16[16,8,128]{2,0,1:T(8,128)(2,1)S(1)}, u32[]{:S(2)}, u32[]{:S(2)}) async-start(bf16[16,8,128]{2,0,1:T(8,128)(2,1)} %copy_bitcast_fusion.6), calls=%async_computation.6 | async-start | bytes 65536 | tf_op jit(solution)/shard_map/all_to_all | solution.py:125
  801.0 20.1 %copy-start.2 = (f32[128,1,8,128]{3,0,2,1:T(8,128)S(1)}, f32[128,1,8,128]{3,0,2,1:T(8,128)}, u32[]{:S(2)}) copy-start(f32[128,1,8,128]{3,0,2,1:T(8,128)} %get-tuple-element.556) | copy-start | bytes 1572868
  806.7 9.8 all-to-all-start.7
  816.5 9.8 all-to-all-start.6
  826.4 10.6 all-to-all-start.5
Sparse Core Ops, SparseCore 0:
  9.9 67.7 all-gather.4
  79.6 63.3 all-gather.6
  792.7 145.2 reduce-scatter.4
  940.5 116.7 reduce-scatter.2
where the time goes:
time: 1080 us; the launch traced here: 1070 us
  other arithmetic  605 us (56%)
  waiting for transfers between devices  276 us (26%)
  local copies, waits for them, and re-layouts  79.1 us (7%)
  starting transfers between devices  36.8 us (3%)
  matrix products  30.4 us (3%)
  loops' own time  23.2 us (2%)
  between operations  14.8 us (1%)
    gather x320, other arithmetic, key_places(): return block_index[row_ids // block_len] * block_len + row_ids % block_len  296 us
    reduce_min x8, other arithmetic, grads_block(): jnp.min(key_place) <= latest_place  135 us
    reduce_min x8, other arithmetic, stats_block(): jnp.min(key_place) <= latest_place  135 us
    reduce_scatter x1, waiting for transfers between devices, body(): lax.psum_scatter(key_grad_all, 'ctx', scatter_dimension=0, tiled=True)  118 us
    reduce_scatter x1, waiting for transfers between devices, body(): lax.psum_scatter(value_grad_all, 'ctx', scatter_dimension=0, tiled=True)  100 us
    gather x32, local copies, waits for them, and re-layouts, key_places(): return block_index[row_ids // block_len] * block_len + row_ids % block_len  23 us
    squeeze x24, local copies, waits for them, and re-layouts, body(): carried, unused = lax.scan(stats_visit, carried, (sub_parts, sub_first))  22.1 us
  transfers between devices with their start and end apart: 12, of which 11 were waited for; matrix products, arithmetic and copies ran while one was open for 29% of the time, Pallas kernels for 0%

commit v1 on v0

v1 whole, which is shorter than its diff:
```python
import functools

import jax
import jax.numpy as jnp
from jax import lax
from jax.experimental import pallas as pl
from jax.experimental.pallas import tpu as pltpu
from jax.sharding import PartitionSpec as P

MESH = pl.DeviceIdType.MESH
F32, BF16 = jnp.float32, jnp.bfloat16
HD = 128
GROUP = 8
BLK = 128
NZ = 8
QW = GROUP * BLK
CK = 4 * BLK
QT = 512
SCALE = HD ** -0.5
EXP_SCALE = SCALE * 1.4426950408889634
LOW = -1e30
NEG = float("-inf")
DEAD = 1 << 20


def dot(a, b):
    return jnp.dot(a, b, preferred_element_type=F32)


def kernel(
    nresp,
    len_ref, row_ref, bi_ref,
    pq, pk, pv, pout, pdo, sq, sk, sv, sout, sdo,
    dqp, dkp, dvp, dqr, dkr, dvr,
    kall, vall, rq, rdo, rk, rv, rdel, dbuf,
    qa, doa, qT, doT, pt, own_pt, mh, mrun, lrun, delta, dqT, psc, dssc,
    gpart, grecv, kept, ysb, yrb, zsb, zrb, dqrows, dkrows, dvrows,
    kzs, kzr, kys, kyr, kcs, kcr, vzs, vzr, vys, vyr, vcs, vcr,
    as_, ar_, gcs, gcr, gys, gyr, gzs, gzr, bs_, br_, loc,
):
    c = lax.axis_index("ctx")
    r = lax.axis_index("resp")
    z = c // 4
    lane4 = c % 4
    core = c % 2
    ylo = lane4 // 2
    cpart = c + 1 - 2 * core
    ypart = c + 2 - 4 * ylo

    def zpeer(d):
        return lax.rem(z + d, NZ) * 4 + lane4

    def rpeer(d):
        return lax.rem(r + d, nresp)

    def remote(src, dst, ss, rs, dev):
        return pltpu.make_async_remote_copy(
            src_ref=src, dst_ref=dst, send_sem=ss, recv_sem=rs, device_id=dev, device_id_type=MESH
        )

    def blk(ref, b):
        return ref.at[pl.ds(pl.multiple_of(b * BLK, BLK), BLK), :]

    def zoff(i):
        return jnp.where(i % 2 == 1, (i + 1) // 2, (NZ - i // 2) % NZ)

    barrier = pltpu.get_barrier_semaphore()

    def greet(dev):
        pl.semaphore_signal(barrier, inc=1, device_id=dev, device_id_type=MESH)

    def greet_z(d, carry):
        greet((zpeer(d), r))
        return carry

    def greet_r(d, carry):
        greet((c, rpeer(d)))
        return carry

    lax.fori_loop(1, NZ, greet_z, 0)
    lax.fori_loop(1, nresp, greet_r, 0)
    greet((cpart, r))
    greet((ypart, r))
    pl.semaphore_wait(barrier, (NZ - 1) + (nresp - 1) + 2)

    def z_copy(src, dst, ss, rs, d):
        return remote(src, blk(dst, c), ss.at[d], rs.at[NZ - d], (zpeer(d), r))

    def z_wait(dst, ss, rs, d):
        b = zpeer(d)
        remote(blk(dst, b), blk(dst, b), ss.at[d], rs.at[d], (b, r)).wait_recv()

    def y_copy(dst, ss, rs, d):
        b = zpeer(d)
        return remote(blk(dst, b), blk(dst, b), ss.at[d], rs.at[d], (ypart, r))

    def y_wait(dst, ss, rs, d):
        b = zpeer(d) + 2 - 4 * ylo
        remote(blk(dst, b), blk(dst, b), ss.at[d], rs.at[d], (ypart, r)).wait_recv()

    def c_copy(dst, ss, rs, d, far):
        b = zpeer(d) + far * (2 - 4 * ylo)
        return remote(blk(dst, b), blk(dst, b), ss.at[d, far], rs.at[d, far], (cpart, r))

    def c_wait(dst, ss, rs, d, far):
        b = zpeer(d) + 1 - 2 * core + far * (2 - 4 * ylo)
        remote(blk(dst, b), blk(dst, b), ss.at[d, far], rs.at[d, far], (cpart, r)).wait_recv()

    ksems = (kzs, kzr, kys, kyr, kcs, kcr)
    vsems = (vzs, vzr, vys, vyr, vcs, vcr)

    def send_own(src, dst, sems):
        zs, zr, ys, yr, cs, cr = sems

        def send(d, carry):
            z_copy(src, dst, zs, zr, d).start()
            return carry

        lax.fori_loop(1, NZ, send, 0)
        dst[pl.ds(pl.multiple_of(c * BLK, BLK), BLK), :] = src[...]
        y_copy(dst, ys, yr, 0).start()
        c_copy(dst, cs, cr, 0, 0).start()

    def pass_on(dst, sems, i):
        zs, zr, ys, yr, cs, cr = sems

        @pl.when(i < NZ)
        def _():
            d = zoff(i)
            z_wait(dst, zs, zr, d)
            y_copy(dst, ys, yr, d).start()
            c_copy(dst, cs, cr, d, 0).start()

    def arrive(dst, sems, i):
        zs, zr, ys, yr, cs, cr = sems
        d = zoff(i)
        y_wait(dst, ys, yr, d)
        c_copy(dst, cs, cr, d, 1).start()
        pass_on(dst, sems, i + 1)
        c_wait(dst, cs, cr, d, 0)
        c_wait(dst, cs, cr, d, 1)

    def drain_gather(src, dst, sems):
        zs, zr, ys, yr, cs, cr = sems

        def drain_z(d, carry):
            z_copy(src, dst, zs, zr, d).wait_send()
            return carry

        def drain_rest(d, carry):
            y_copy(dst, ys, yr, d).wait_send()
            c_copy(dst, cs, cr, d, 0).wait_send()
            c_copy(dst, cs, cr, d, 1).wait_send()
            return carry

        lax.fori_loop(1, NZ, drain_z, 0)
        lax.fori_loop(0, NZ, drain_rest, 0)

    def cols(ref, p, w):
        return ref.at[:, pl.ds(pl.multiple_of(p * w, 128), w)]

    def slots(ref, p):
        return ref.at[pl.ds(pl.multiple_of(p * 16, 16), 16), :]

    def sources(p):
        return (cols(sq, p, QW), cols(sdo, p, QW), cols(sk, p, HD), cols(sv, p, HD), dbuf.at[p])

    landings = (rq, rdo, rk, rv, rdel)

    def exchange(d, which):
        p = rpeer(d)
        src = sources(p)
        return [
            remote(src[n], slots(landings[n], r), as_.at[n, d], ar_.at[n, nresp - d], (c, p))
            for n in which
        ]

    def exchange_in(d):
        p = rpeer(d)
        return [
            remote(slots(landings[n], p), slots(landings[n], p), as_.at[n, d], ar_.at[n, d], (c, p))
            for n in range(5)
        ]

    def local_in(which):
        src = sources(r)
        return [pltpu.make_async_copy(src[n], slots(landings[n], r), loc.at[n]) for n in which]

    send_own(pk, kall, ksems)

    def send_qdo(d, carry):
        for cp in exchange(d, range(4)):
            cp.start()
        return carry

    lax.fori_loop(1, nresp, send_qdo, 0)
    for cp in local_in(range(4)):
        cp.start()
    send_own(pv, vall, vsems)

    lane16 = lax.broadcasted_iota(jnp.int32, (16, 128), 1)
    for g in range(nresp):
        acc = jnp.zeros((16, 128), F32)
        for h in range(GROUP):
            sl = slice((g * GROUP + h) * HD, (g * GROUP + h + 1) * HD)
            prod = sout[:, sl].astype(F32) * sdo[:, sl].astype(F32)
            acc = jnp.where(lane16 == h, jnp.sum(prod, axis=1, keepdims=True), acc)
        dbuf[g] = acc

    def send_delta(d, carry):
        exchange(d, (4,))[0].start()
        return carry

    lax.fori_loop(1, nresp, send_delta, 0)
    local_in((4,))[0].start()

    lane = lax.broadcasted_iota(jnp.int32, (128, 128), 1)
    subl = lax.broadcasted_iota(jnp.int32, (128, 128), 0)
    diff = lane - subl
    my = bi_ref[c]

    def load_queries(q, do, base):
        for h in range(GROUP):
            sl = slice(h * HD, (h + 1) * HD)
            out = slice(base + h * BLK, base + (h + 1) * BLK)
            qh, dh = q[:, sl], do[:, sl]
            qa[out, :] = qh
            doa[out, :] = dh
            qT[:, out] = qh.T
            doT[:, out] = dh.T

    def place_delta(rows, base):
        rows_t = rows.T
        for h in range(GROUP):
            delta[:, base + h * BLK: base + (h + 1) * BLK] = rows_t[h:h + 1, :]

    load_queries(pq, pdo, 0)
    acc = jnp.zeros((BLK, 128), F32)
    for h in range(GROUP):
        sl = slice(h * HD, (h + 1) * HD)
        prod = pout[:, sl].astype(F32) * pdo[:, sl].astype(F32)
        acc = jnp.where(lane == h, jnp.sum(prod, axis=1, keepdims=True), acc)
    place_delta(acc, 0)
    mrun[...] = jnp.full((1, 2 * QW), LOW, F32)
    lrun[...] = jnp.zeros((1, 2 * QW), F32)

    def stats_chunk(i, base, masked):
        zc = lax.rem(z + zoff(i), NZ)
        kc = kall[pl.ds(pl.multiple_of(zc * CK, CK), CK), :]
        prow = pl.ds(pl.multiple_of(i * CK, CK), CK)
        if masked:
            masks = [diff >= (bi_ref[zc * 4 + b] - my) * BLK for b in range(4)]
            masks = [jnp.concatenate([mk] * (QT // BLK), axis=1) for mk in masks]
        for t in range(QW // QT):
            sl = slice(base + t * QT, base + (t + 1) * QT)
            s = dot(kc, qT[:, sl])
            if masked:
                s = jnp.concatenate(
                    [jnp.where(masks[b], s[b * BLK:(b + 1) * BLK, :], NEG) for b in range(4)], axis=0
                )
            mo = mrun[:, sl]
            m = jnp.maximum(mo, jnp.max(s, axis=0, keepdims=True))
            p = jnp.exp2((s - m) * EXP_SCALE)
            pt[prow, sl] = p.astype(BF16)
            mrun[:, sl] = m
            mh[pl.ds(i, 1), sl] = m
            lrun[:, sl] = lrun[:, sl] * jnp.exp2((mo - m) * EXP_SCALE) + jnp.sum(p, axis=0, keepdims=True)

    def prompt_stats(i, carry):
        arrive(kall, ksems, i)
        stats_chunk(i, 0, True)
        return carry

    lax.fori_loop(0, NZ, prompt_stats, 0)

    def wait_in(d, carry):
        for cp in exchange_in(d):
            cp.wait_recv()
        return carry

    lax.fori_loop(1, nresp, wait_in, 0)
    for cp in local_in(range(5)):
        cp.wait()
    load_queries(rq, rdo, QW)
    place_delta(rdel[...], QW)

    lane1 = lax.broadcasted_iota(jnp.int32, (1, 128), 1)
    startq = jnp.full((1, 128), DEAD, jnp.int32)
    cum = jnp.int32(0)
    for n in range(len_ref.shape[0]):
        count = jnp.where(row_ref[n] == c, len_ref[n], 0)
        startq = jnp.where((lane1 >= cum) & (lane1 < cum + count), cum, startq)
        cum = cum + count
    live = jnp.where(startq < DEAD, 1.0, 0.0)
    own_mask = (subl >= startq) & (diff >= 0)
    for h in range(GROUP):
        sl = slice(QW + h * BLK, QW + (h + 1) * BLK)
        s = jnp.where(own_mask, dot(rk[...], qT[:, sl]), NEG)
        m = jnp.maximum(jnp.max(s, axis=0, keepdims=True), LOW)
        p = jnp.exp2((s - m) * EXP_SCALE)
        own_pt[:, h * BLK:(h + 1) * BLK] = p.astype(BF16)
        mh[NZ:NZ + 1, sl] = m
        mrun[:, sl] = m
        lrun[:, sl] = jnp.sum(p, axis=0, keepdims=True)

    def resp_stats(i, carry):
        arrive(vall, vsems, i)
        stats_chunk(i, QW, False)
        return carry

    lax.fori_loop(0, NZ, resp_stats, 0)

    total = lrun[...]
    inv = jnp.where(total > 0.0, 1.0 / total, 0.0)
    inv = inv * jnp.concatenate([jnp.ones((1, QW), F32)] + [live] * GROUP, axis=1)
    mh[0:NZ, :] = jnp.exp2((mh[0:NZ, :] - mrun[...]) * EXP_SCALE) * inv
    own_f = jnp.exp2((mh[NZ:NZ + 1, QW:] - mrun[:, QW:]) * EXP_SCALE) * inv[:, QW:]
    dqT[...] = jnp.zeros_like(dqT)

    def core_send(j):
        return remote(gpart.at[j, 1 - core], grecv.at[j], gcs.at[j], gcr.at[j], (cpart, r))

    def y_send(j):
        return remote(ysb.at[j], yrb.at[j], gys.at[j], gyr.at[j], (ypart, r))

    def z_send(j):
        d = zoff(NZ - 1 - j)
        return remote(zsb.at[j], zrb.at[NZ - d], gzs.at[d], gzr.at[NZ - d], (zpeer(d), r))

    def after_core(j):
        core_send(j).wait_recv()
        kept[j] = gpart[j, core, ylo] + grecv[j, ylo]
        ysb[j] = (gpart[j, core, 1 - ylo] + grecv[j, 1 - ylo]).astype(BF16)
        y_send(j).start()

    def after_y(j):
        y_send(j).wait_recv()
        zsb[j] = (kept[j] + yrb[j].astype(F32)).astype(BF16)
        z_send(j).start()

    def grads(j, carry):
        i = NZ - 1 - j
        zc = lax.rem(z + zoff(i), NZ)
        krow = pl.ds(pl.multiple_of(zc * CK, CK), CK)
        prow = pl.ds(pl.multiple_of(i * CK, CK), CK)
        vc = vall[krow, :]
        kTc = kall[krow, :].T
        f = mh[pl.ds(i, 1), :]
        for t in range(2 * QW // QT):
            sl = slice(t * QT, (t + 1) * QT)
            dp = dot(vc, doT[:, sl])
            p = pt[prow, sl].astype(F32) * f[:, sl]
            ds = (p * (dp - delta[:, sl])).astype(BF16)
            psc[:, sl] = p.astype(BF16)
            dssc[:, sl] = ds
            dqT[:, sl] += dot(kTc, ds)
        dk = dot(dssc[...], qa[...])
        dv = dot(psc[...], doa[...])
        for b in range(4):
            gpart[j, b % 2, b // 2, 0] = dk[b * BLK:(b + 1) * BLK, :]
            gpart[j, b % 2, b // 2, 1] = dv[b * BLK:(b + 1) * BLK, :]
        core_send(j).start()

        @pl.when(j >= 1)
        def _():
            after_core(j - 1)

        @pl.when(j >= 2)
        def _():
            after_y(j - 2)

        return carry

    lax.fori_loop(0, NZ, grads, 0)

    rkT = rk[...].T
    for h in range(GROUP):
        sl = slice(QW + h * BLK, QW + (h + 1) * BLK)
        dp = dot(rv[...], doT[:, sl])
        p = own_pt[:, h * BLK:(h + 1) * BLK].astype(F32) * own_f[:, h * BLK:(h + 1) * BLK]
        ds = (p * (dp - delta[:, sl])).astype(BF16)
        psc[0:BLK, sl] = p.astype(BF16)
        dssc[0:BLK, sl] = ds
        dqT[:, sl] += dot(rkT, ds)
    dvrows[...] = dot(psc[0:BLK, QW:], doa[QW:, :]).astype(BF16)
    dkrows[...] = (dot(dssc[0:BLK, QW:], qa[QW:, :]) * SCALE).astype(BF16)
    for h in range(GROUP):
        dqrows[:, h * HD:(h + 1) * HD] = (dqT[:, QW + h * BLK:QW + (h + 1) * BLK].T * SCALE).astype(BF16)

    def back(d):
        p = rpeer(d)
        dev = (c, p)
        e = nresp - d
        return (
            remote(slots(dqrows, p), cols(dqr, r, QW), bs_.at[0, d], br_.at[0, e], dev),
            remote(slots(dkrows, p), cols(dkr, r, HD), bs_.at[1, d], br_.at[1, e], dev),
            remote(slots(dvrows, p), cols(dvr, r, HD), bs_.at[2, d], br_.at[2, e], dev),
        )

    def back_in(d):
        p = rpeer(d)
        dev = (c, p)
        return (
            remote(cols(dqr, p, QW), cols(dqr, p, QW), bs_.at[0, d], br_.at[0, d], dev),
            remote(cols(dkr, p, HD), cols(dkr, p, HD), bs_.at[1, d], br_.at[1, d], dev),
            remote(cols(dvr, p, HD), cols(dvr, p, HD), bs_.at[2, d], br_.at[2, d], dev),
        )

    def local_back():
        return (
            pltpu.make_async_copy(slots(dqrows, r), cols(dqr, r, QW), loc.at[5]),
            pltpu.make_async_copy(slots(dkrows, r), cols(dkr, r, HD), loc.at[6]),
            pltpu.make_async_copy(slots(dvrows, r), cols(dvr, r, HD), loc.at[7]),
        )

    def send_back(d, carry):
        for cp in back(d):
            cp.start()
        return carry

    lax.fori_loop(1, nresp, send_back, 0)
    for cp in local_back():
        cp.start()

    after_core(NZ - 1)
    after_y(NZ - 2)
    for h in range(GROUP):
        dqp[:, h * HD:(h + 1) * HD] = (dqT[:, h * BLK:(h + 1) * BLK].T * SCALE).astype(BF16)
    y_send(NZ - 1).wait_recv()
    kept[NZ - 1] = kept[NZ - 1] + yrb[NZ - 1].astype(F32)

    drain_gather(pk, kall, ksems)
    drain_gather(pv, vall, vsems)

    def drain_exchange(d, carry):
        for cp in exchange(d, range(5)):
            cp.wait_send()
        return carry

    lax.fori_loop(1, nresp, drain_exchange, 0)

    def drain_parts(j, carry):
        core_send(j).wait_send()
        y_send(j).wait_send()
        return carry

    lax.fori_loop(0, NZ, drain_parts, 0)

    def drain_z(j, carry):
        z_send(j).wait_send()
        return carry

    lax.fori_loop(0, NZ - 1, drain_z, 0)

    def z_parts(d, carry):
        remote(zrb.at[d], zrb.at[d], gzs.at[d], gzr.at[d], (zpeer(d), r)).wait_recv()
        kept[NZ - 1] = kept[NZ - 1] + zrb[d].astype(F32)
        return carry

    lax.fori_loop(1, NZ, z_parts, 0)
    dkp[...] = (kept[NZ - 1, 0] * SCALE).astype(BF16)
    dvp[...] = kept[NZ - 1, 1].astype(BF16)

    def finish_back(d, carry):
        for cp in back(d):
            cp.wait_send()
        for cp in back_in(d):
            cp.wait_recv()
        return carry

    lax.fori_loop(1, nresp, finish_back, 0)
    for cp in local_back():
        cp.wait()


def solution(mesh):
    nresp = mesh.shape["resp"]
    keys = mesh.shape["ctx"] * BLK

    def body(
        prompt_q, prompt_k, prompt_v, prompt_out, prompt_dout,
        resp_q, resp_k, resp_v, resp_out, resp_dout,
        lengths, resp_row, block_index,
    ):
        shape = jax.ShapeDtypeStruct
        smem = pl.BlockSpec(memory_space=pltpu.SMEM)
        vmem = pl.BlockSpec(memory_space=pltpu.VMEM)
        dma = pltpu.SemaphoreType.DMA
        own = prompt_q.shape[0]
        gather_sems = [dma((NZ,)), dma((NZ,)), dma((NZ,)), dma((NZ,)), dma((NZ, 2)), dma((NZ, 2))]
        return pl.pallas_call(
            functools.partial(kernel, nresp),
            out_shape=(
                shape(prompt_q.shape, BF16),
                shape(prompt_k.shape, BF16),
                shape(prompt_v.shape, BF16),
                shape(resp_q.shape, BF16),
                shape(resp_k.shape, BF16),
                shape(resp_v.shape, BF16),
            ),
            in_specs=[smem] * 3 + [vmem] * 10,
            out_specs=(vmem,) * 6,
            scratch_shapes=[
                pltpu.VMEM((keys, HD), BF16),
                pltpu.VMEM((keys, HD), BF16),
                pltpu.VMEM((own, QW), BF16),
                pltpu.VMEM((own, QW), BF16),
                pltpu.VMEM((own, HD), BF16),
                pltpu.VMEM((own, HD), BF16),
                pltpu.VMEM((own, 128), F32),
                pltpu.VMEM((nresp, 16, 128), F32),
                pltpu.VMEM((2 * QW, HD), BF16),
                pltpu.VMEM((2 * QW, HD), BF16),
                pltpu.VMEM((HD, 2 * QW), BF16),
                pltpu.VMEM((HD, 2 * QW), BF16),
                pltpu.VMEM((keys, 2 * QW), BF16),
                pltpu.VMEM((BLK, QW), BF16),
                pltpu.VMEM((2 * NZ, 2 * QW), F32),
                pltpu.VMEM((1, 2 * QW), F32),
                pltpu.VMEM((1, 2 * QW), F32),
                pltpu.VMEM((1, 2 * QW), F32),
                pltpu.VMEM((HD, 2 * QW), F32),
                pltpu.VMEM((CK, 2 * QW), BF16),
                pltpu.VMEM((CK, 2 * QW), BF16),
                pltpu.VMEM((NZ, 2, 2, 2, BLK, HD), F32),
                pltpu.VMEM((NZ, 2, 2, BLK, HD), F32),
                pltpu.VMEM((NZ, 2, BLK, HD), F32),
                pltpu.VMEM((NZ, 2, BLK, HD), BF16),
                pltpu.VMEM((NZ, 2, BLK, HD), BF16),
                pltpu.VMEM((NZ, 2, BLK, HD), BF16),
                pltpu.VMEM((NZ, 2, BLK, HD), BF16),
                pltpu.VMEM((own, QW), BF16),
                pltpu.VMEM((own, HD), BF16),
                pltpu.VMEM((own, HD), BF16),
            ]
            + gather_sems
            + gather_sems
            + [
                dma((5, nresp)),
                dma((5, nresp)),
                dma((NZ,)),
                dma((NZ,)),
                dma((NZ,)),
                dma((NZ,)),
                dma((NZ,)),
                dma((NZ,)),
                dma((3, nresp)),
                dma((3, nresp)),
                dma((8,)),
            ],
            compiler_params=pltpu.CompilerParams(
                collective_id=0, has_side_effects=True, vmem_limit_bytes=60 * 1024 * 1024
            ),
            name="attn_bwd",
        )(
            lengths, resp_row, block_index,
            prompt_q, prompt_k, prompt_v, prompt_out, prompt_dout,
            resp_q, resp_k, resp_v, resp_out, resp_dout,
        )

    heads, rows, whole = P("ctx", "resp"), P(("ctx", "resp"), None), P()
    return jax.shard_map(
        body,
        mesh=mesh,
        in_specs=(heads,) * 5 + (rows,) * 5 + (whole,) * 3,
        out_specs=(heads,) * 3 + (rows,) * 3,
        check_vma=False,
    )
```

time: 1080 us -> 105 us (0.10); the launches traced: 1070 us -> 104 us
  other arithmetic: 605 us -> 0 us
  waiting for transfers between devices: 276 us -> 0 us
  Pallas kernels: 0 us -> 97.9 us
  local copies, waits for them, and re-layouts: 79.1 us -> 5.25 us
  starting transfers between devices: 36.8 us -> 0 us
  matrix products: 30.4 us -> 0 us
  loops' own time: 23.2 us -> 0 us
  between operations: 14.8 us -> 0.67 us
    gather x320 -> x0, other arithmetic: 296 us -> none  [key_places(): return block_index[row_ids // block_len] * block_len + row_ids % block_len]
    reduce_min x16 -> x0, other arithmetic: 270 us -> none  [the longest x8 135 us: grads_block(): jnp.min(key_place) <= latest_place]
    reduce_scatter x2 -> x0, waiting for transfers between devices: 218 us -> none  [the longest x1 118 us: body(): lax.psum_scatter(key_grad_all, 'ctx', scatter_dimension=0, tiled=True)]
    pallas_call x0 -> x1, Pallas kernels: none -> 97.9 us  [body(): pl.pallas_call(functools.partial(kernel, nresp), out_shape=(shape(prompt_...]
    all_to_all x8 -> x0, waiting for transfers between devices: 38.2 us -> none  [the longest x1 6.37 us: body(): lax.all_to_all(resp_dout, 'resp', split_axis=1, concat_axis=0, tiled=True)]
    all_to_all x8 -> x0, starting transfers between devices: 36.6 us -> none  [the longest x1 7.48 us: body(): lax.all_to_all(resp_out, 'resp', split_axis=1, concat_axis=0, tiled=True)]
    dot_general x53 -> x0, matrix products: 30.4 us -> none  [the longest x17 13.8 us: masked_scores(): jnp.einsum('qhgd,khd->hgqk', queries, key_rows, preferred_element_type=jn...]
    another operation x34 -> x0, loops' own time: 23.2 us -> none  [the longest x1 10.9 us: body(): lax.scan(grads_visit, query_sums, (sub_keys, sub_values, sub_first))]
  transfers between devices with their start and end apart: 12 -> 0, of which waited for: 11 -> 0; matrix products, arithmetic and copies ran while one was open for 29% -> 0% of each run, Pallas kernels for 0% -> 0%
where the time goes in v1:
time: 105 us; the launch traced here: 104 us
  Pallas kernels  97.9 us (93%)
  local copies, waits for them, and re-layouts  5.25 us (5%)
    pallas_call x1, Pallas kernels, body(): pl.pallas_call(functools.partial(kernel, nresp), out_shape=(shape(prompt_...  97.9 us
    unnamed x16, local copies, waits for them, and re-layouts  5.25 us

profile of v1, /device:TPU:1, one launch (start us, length us, event | category | flops | bytes accessed | tf_op | source)
XLA Modules:
  0.0 103.8 jit_solution(14781887242502958619)
XLA Ops:
  0.6 97.9 %attn_bwd.1 = (bf16[128,1024]{1,0:T(8,128)(2,1)}, bf16[128,128]{1,0:T(8,128)(2,1)}, bf16[128,128]{1,0:T(8,128)(2,1)}, bf16[16,8192]{1,0:T(8,128)(2,1)}, bf16[16,...) custom-call(s32[16]{0:T(128)} %len_ref.1, s32[16]{0:T(128)} %row_ref.1, s32[32]{0:T(128)} %bi_ref.1, bf16[128,1024]{1,0:T(8,128)(2,1)} %pq.1, ...), custom_call_target="tpu_custom_call" | custom-call | tf_op jit(solution)/shard_map/attn_bwd/pallas_call | solution.py:491
  98.5 0.0 copy-start.4
  98.6 0.0 copy-start
  98.6 1.7 %copy.25 = bf16[128,1024]{1,0:T(8,128)(2,1)} copy(bf16[128,1024]{1,0:T(8,128)(2,1)} %get-tuple-element.12) | data formatting | bytes 524288
  100.3 0.0 copy-done.4
  100.3 0.0 copy-start.3
  100.3 0.6 copy.26
  100.9 0.2 copy-done.3
  101.0 0.6 copy.27
  101.7 0.0 copy-done
  101.7 0.0 copy-start.2
  101.7 0.7 copy.28
  102.4 0.1 copy-done.2
  102.4 0.0 copy-start.1
  102.4 0.6 copy.29
  103.0 0.2 copy-done.1
  103.2 0.6 copy.30
Async XLA Ops:
  98.5 1.7 %copy-start.4 = (bf16[128,128]{1,0:T(8,128)(2,1)S(1)}, bf16[128,128]{1,0:T(8,128)(2,1)}, u32[]{:S(2)}) copy-start(bf16[128,128]{1,0:T(8,128)(2,1)} %get-tuple-element.13) | copy-start | bytes 98308
  98.6 3.1 %copy-start = (bf16[16,8192]{1,0:T(8,128)(2,1)S(1)}, bf16[16,8192]{1,0:T(8,128)(2,1)}, u32[]{:S(2)}) copy-start(bf16[16,8192]{1,0:T(8,128)(2,1)} %get-tuple-element.15) | copy-start | bytes 786436
  100.3 0.8 copy-start.3
  101.7 0.8 copy-start.2
  102.4 0.8 copy-start.1

commit v2 on v1

--- a/solution.py
+++ b/solution.py
@@ -13,6 +13,7 @@
 GROUP = 8
 BLK = 128
 NZ = 8
+LEAD = 3
 QW = GROUP * BLK
 CK = 4 * BLK
 QT = 512
@@ -32,10 +33,10 @@
     len_ref, row_ref, bi_ref,
     pq, pk, pv, pout, pdo, sq, sk, sv, sout, sdo,
     dqp, dkp, dvp, dqr, dkr, dvr,
-    kall, vall, rq, rdo, rk, rv, rdel, dbuf,
+    kv, rq, rdo, rk, rv, rdel, dbuf,
     qa, doa, qT, doT, pt, own_pt, mh, mrun, lrun, delta, dqT, psc, dssc,
     gpart, grecv, kept, ysb, yrb, zsb, zrb, dqrows, dkrows, dvrows,
-    kzs, kzr, kys, kyr, kcs, kcr, vzs, vzr, vys, vyr, vcs, vcr,
+    zs, zr, ys, yr, cs, cr,
     as_, ar_, gcs, gcr, gys, gyr, gzs, gzr, bs_, br_, loc,
 ):
     c = lax.axis_index("ctx")
@@ -58,9 +59,6 @@
             src_ref=src, dst_ref=dst, send_sem=ss, recv_sem=rs, device_id=dev, device_id_type=MESH
         )
 
-    def blk(ref, b):
-        return ref.at[pl.ds(pl.multiple_of(b * BLK, BLK), BLK), :]
-
     def zoff(i):
         return jnp.where(i % 2 == 1, (i + 1) // 2, (NZ - i // 2) % NZ)
 
@@ -83,74 +81,72 @@
     greet((ypart, r))
     pl.semaphore_wait(barrier, (NZ - 1) + (nresp - 1) + 2)
 
-    def z_copy(src, dst, ss, rs, d):
-        return remote(src, blk(dst, c), ss.at[d], rs.at[NZ - d], (zpeer(d), r))
-
-    def z_wait(dst, ss, rs, d):
+    def z_copy(d):
+        return remote(kv.at[c], kv.at[c], zs.at[d], zr.at[NZ - d], (zpeer(d), r))
+
+    def z_wait(d):
         b = zpeer(d)
-        remote(blk(dst, b), blk(dst, b), ss.at[d], rs.at[d], (b, r)).wait_recv()
-
-    def y_copy(dst, ss, rs, d):
+        remote(kv.at[b], kv.at[b], zs.at[d], zr.at[d], (b, r)).wait_recv()
+
+    def y_copy(d):
         b = zpeer(d)
-        return remote(blk(dst, b), blk(dst, b), ss.at[d], rs.at[d], (ypart, r))
-
-    def y_wait(dst, ss, rs, d):
+        return remote(kv.at[b], kv.at[b], ys.at[d], yr.at[d], (ypart, r))
+
+    def y_wait(d):
         b = zpeer(d) + 2 - 4 * ylo
-        remote(blk(dst, b), blk(dst, b), ss.at[d], rs.at[d], (ypart, r)).wait_recv()
-
-    def c_copy(dst, ss, rs, d, far):
+        remote(kv.at[b], kv.at[b], ys.at[d], yr.at[d], (ypart, r)).wait_recv()
+
+    def c_copy(d, far):
         b = zpeer(d) + far * (2 - 4 * ylo)
-        return remote(blk(dst, b), blk(dst, b), ss.at[d, far], rs.at[d, far], (cpart, r))
-
-    def c_wait(dst, ss, rs, d, far):
+        return remote(kv.at[b], kv.at[b], cs.at[d, far], cr.at[d, far], (cpart, r))
+
+    def c_wait(d, far):
         b = zpeer(d) + 1 - 2 * core + far * (2 - 4 * ylo)
-        remote(blk(dst, b), blk(dst, b), ss.at[d, far], rs.at[d, far], (cpart, r)).wait_recv()
-
-    ksems = (kzs, kzr, kys, kyr, kcs, kcr)
-    vsems = (vzs, vzr, vys, vyr, vcs, vcr)
-
-    def send_own(src, dst, sems):
-        zs, zr, ys, yr, cs, cr = sems
-
-        def send(d, carry):
-            z_copy(src, dst, zs, zr, d).start()
+        remote(kv.at[b], kv.at[b], cs.at[d, far], cr.at[d, far], (cpart, r)).wait_recv()
+
+    def send_own():
+        kv[c, 0] = pk[...]
+        kv[c, 1] = pv[...]
+        y_copy(0).start()
+        c_copy(0, 0).start()
+
+        def send(i, carry):
+            z_copy(zoff(i)).start()
             return carry
 
         lax.fori_loop(1, NZ, send, 0)
-        dst[pl.ds(pl.multiple_of(c * BLK, BLK), BLK), :] = src[...]
-        y_copy(dst, ys, yr, 0).start()
-        c_copy(dst, cs, cr, 0, 0).start()
-
-    def pass_on(dst, sems, i):
-        zs, zr, ys, yr, cs, cr = sems
-
+
+    def pass_near(i):
         @pl.when(i < NZ)
         def _():
             d = zoff(i)
-            z_wait(dst, zs, zr, d)
-            y_copy(dst, ys, yr, d).start()
-            c_copy(dst, cs, cr, d, 0).start()
-
-    def arrive(dst, sems, i):
-        zs, zr, ys, yr, cs, cr = sems
+            z_wait(d)
+            y_copy(d).start()
+            c_copy(d, 0).start()
+
+    def pass_far(i):
+        @pl.when(i < NZ)
+        def _():
+            d = zoff(i)
+            y_wait(d)
+            c_copy(d, 1).start()
+
+    def arrive(i):
+        pass_near(i + LEAD + 1)
+        pass_far(i + 1)
         d = zoff(i)
-        y_wait(dst, ys, yr, d)
-        c_copy(dst, cs, cr, d, 1).start()
-        pass_on(dst, sems, i + 1)
-        c_wait(dst, cs, cr, d, 0)
-        c_wait(dst, cs, cr, d, 1)
-
-    def drain_gather(src, dst, sems):
-        zs, zr, ys, yr, cs, cr = sems
-
+        c_wait(d, 0)
+        c_wait(d, 1)
+
+    def drain_gather():
         def drain_z(d, carry):
-            z_copy(src, dst, zs, zr, d).wait_send()
+            z_copy(d).wait_send()
             return carry
 
         def drain_rest(d, carry):
-            y_copy(dst, ys, yr, d).wait_send()
-            c_copy(dst, cs, cr, d, 0).wait_send()
-            c_copy(dst, cs, cr, d, 1).wait_send()
+            y_copy(d).wait_send()
+            c_copy(d, 0).wait_send()
+            c_copy(d, 1).wait_send()
             return carry
 
         lax.fori_loop(1, NZ, drain_z, 0)
@@ -186,7 +182,7 @@
         src = sources(r)
         return [pltpu.make_async_copy(src[n], slots(landings[n], r), loc.at[n]) for n in which]
 
-    send_own(pk, kall, ksems)
+    send_own()
 
     def send_qdo(d, carry):
         for cp in exchange(d, range(4)):
@@ -196,7 +192,6 @@
     lax.fori_loop(1, nresp, send_qdo, 0)
     for cp in local_in(range(4)):
         cp.start()
-    send_own(pv, vall, vsems)
 
     lane16 = lax.broadcasted_iota(jnp.int32, (16, 128), 1)
     for g in range(nresp):
@@ -246,7 +241,7 @@
 
     def stats_chunk(i, base, masked):
         zc = lax.rem(z + zoff(i), NZ)
-        kc = kall[pl.ds(pl.multiple_of(zc * CK, CK), CK), :]
+        kc = kv[pl.ds(zc * 4, 4), 0].reshape(CK, HD)
         prow = pl.ds(pl.multiple_of(i * CK, CK), CK)
         if masked:
             masks = [diff >= (bi_ref[zc * 4 + b] - my) * BLK for b in range(4)]
@@ -266,11 +261,17 @@
             mh[pl.ds(i, 1), sl] = m
             lrun[:, sl] = lrun[:, sl] * jnp.exp2((mo - m) * EXP_SCALE) + jnp.sum(p, axis=0, keepdims=True)
 
+    def near_first(i, carry):
+        pass_near(i)
+        return carry
+
     def prompt_stats(i, carry):
-        arrive(kall, ksems, i)
+        arrive(i)
         stats_chunk(i, 0, True)
         return carry
 
+    lax.fori_loop(1, LEAD + 1, near_first, 0)
+    pass_far(0)
     lax.fori_loop(0, NZ, prompt_stats, 0)
 
     def wait_in(d, carry):
@@ -304,7 +305,6 @@
         lrun[:, sl] = jnp.sum(p, axis=0, keepdims=True)
 
     def resp_stats(i, carry):
-        arrive(vall, vsems, i)
         stats_chunk(i, QW, False)
         return carry
 
@@ -341,10 +341,9 @@
     def grads(j, carry):
         i = NZ - 1 - j
         zc = lax.rem(z + zoff(i), NZ)
-        krow = pl.ds(pl.multiple_of(zc * CK, CK), CK)
         prow = pl.ds(pl.multiple_of(i * CK, CK), CK)
-        vc = vall[krow, :]
-        kTc = kall[krow, :].T
+        vc = kv[pl.ds(zc * 4, 4), 1].reshape(CK, HD)
+        kTc = kv[pl.ds(zc * 4, 4), 0].reshape(CK, HD).T
         f = mh[pl.ds(i, 1), :]
         for t in range(2 * QW // QT):
             sl = slice(t * QT, (t + 1) * QT)
@@ -429,8 +428,7 @@
     y_send(NZ - 1).wait_recv()
     kept[NZ - 1] = kept[NZ - 1] + yrb[NZ - 1].astype(F32)
 
-    drain_gather(pk, kall, ksems)
-    drain_gather(pv, vall, vsems)
+    drain_gather()
 
     def drain_exchange(d, carry):
         for cp in exchange(d, range(5)):
@@ -470,6 +468,16 @@
 
     lax.fori_loop(1, nresp, finish_back, 0)
     for cp in local_back():
+        cp.wait()
+
+
+def settle(*refs):
+    n = (len(refs) - 1) // 2
+    sems = refs[-1]
+    copies = [pltpu.make_async_copy(refs[k], refs[n + k], sems.at[k]) for k in range(n)]
+    for cp in copies:
+        cp.start()
+    for cp in copies:
         cp.wait()
 
 
@@ -488,7 +496,7 @@
         dma = pltpu.SemaphoreType.DMA
         own = prompt_q.shape[0]
         gather_sems = [dma((NZ,)), dma((NZ,)), dma((NZ,)), dma((NZ,)), dma((NZ, 2)), dma((NZ, 2))]
-        return pl.pallas_call(
+        parts = pl.pallas_call(
             functools.partial(kernel, nresp),
             out_shape=(
                 shape(prompt_q.shape, BF16),
@@ -501,8 +509,7 @@
             in_specs=[smem] * 3 + [vmem] * 10,
             out_specs=(vmem,) * 6,
             scratch_shapes=[
-                pltpu.VMEM((keys, HD), BF16),
-                pltpu.VMEM((keys, HD), BF16),
+                pltpu.VMEM((keys // BLK, 2, BLK, HD), BF16),
                 pltpu.VMEM((own, QW), BF16),
                 pltpu.VMEM((own, QW), BF16),
                 pltpu.VMEM((own, HD), BF16),
@@ -534,7 +541,6 @@
                 pltpu.VMEM((own, HD), BF16),
             ]
             + gather_sems
-            + gather_sems
             + [
                 dma((5, nresp)),
                 dma((5, nresp)),
@@ -557,6 +563,15 @@
             prompt_q, prompt_k, prompt_v, prompt_out, prompt_dout,
             resp_q, resp_k, resp_v, resp_out, resp_dout,
         )
+        anywhere = pl.BlockSpec(memory_space=pltpu.HBM)
+        return pl.pallas_call(
+            settle,
+            out_shape=tuple(shape(part.shape, part.dtype) for part in parts),
+            in_specs=[anywhere] * 6,
+            out_specs=(anywhere,) * 6,
+            scratch_shapes=[dma((6,))],
+            name="settle",
+        )(*parts)
 
     heads, rows, whole = P("ctx", "resp"), P(("ctx", "resp"), None), P()
     return jax.shard_map(

time: 105 us -> 98.5 us (0.938)
  the two profiles are of different devices: /device:TPU:1 before, /device:TPU:8 now
where the time goes in v2:
time: 98.5 us; the launch traced here: 98.4 us
  Pallas kernels  97.8 us (99%)
    pallas_call x1, Pallas kernels, body(): pl.pallas_call(functools.partial(kernel, nresp), out_shape=(shape(prompt_...  76.8 us
    pallas_call x1, Pallas kernels, body(): pl.pallas_call(settle, out_shape=tuple((shape(part.shape, part.dtype) for...  21 us

profile of v2, /device:TPU:8, one launch (start us, length us, event | category | flops | bytes accessed | tf_op | source)
XLA Modules:
  0.0 98.4 jit_solution(1300594406646908385)
XLA Ops:
  0.6 76.8 %attn_bwd.1 = (bf16[128,1024]{1,0:T(8,128)(2,1)}, bf16[128,128]{1,0:T(8,128)(2,1)}, bf16[128,128]{1,0:T(8,128)(2,1)}, bf16[16,8192]{1,0:T(8,128)(2,1)}, bf16[16,...) custom-call(s32[16]{0:T(128)} %len_ref.1, s32[16]{0:T(128)} %row_ref.1, s32[32]{0:T(128)} %bi_ref.1, bf16[128,1024]{1,0:T(8,128)(2,1)} %pq.1, ...), custom_call_target="tpu_custom_call" | custom-call | tf_op jit(solution)/shard_map/attn_bwd/pallas_call | solution.py:499
  77.4 21.0 %settle.1 = (bf16[128,1024]{1,0:T(8,128)(2,1)}, bf16[128,128]{1,0:T(8,128)(2,1)}, bf16[128,128]{1,0:T(8,128)(2,1)}, bf16[16,8192]{1,0:T(8,128)(2,1)}, bf16[16,10...) custom-call(bf16[128,1024]{1,0:T(8,128)(2,1)} %get-tuple-element.12.refs_0_, bf16[128,128]{1,0:T(8,128)(2,1)} %get-tuple-element.13.refs_1_, ...), custom_call_target="tpu_custom_call" | custom-call | tf_op jit(solution)/shard_map/settle/pallas_call | solution.py:567

commit v3 on v2

v3 whole, which is shorter than its diff:
```python
import functools

import jax
import jax.numpy as jnp
from jax import lax
from jax.experimental import pallas as pl
from jax.experimental.pallas import tpu as pltpu
from jax.sharding import PartitionSpec as P

MESH = pl.DeviceIdType.MESH
F32, BF16 = jnp.float32, jnp.bfloat16
HD = 128
GROUP = 8
BLK = 128
NZ = 8
LEAD = 3
QW = GROUP * BLK
CK = 4 * BLK
QT = 512
SCALE = HD ** -0.5
EXP_SCALE = SCALE * 1.4426950408889634
LOW = -1e30
NEG = float("-inf")
DEAD = 1 << 20


def dot(a, b):
    return jnp.dot(a, b, preferred_element_type=F32)


def kernel(
    nresp,
    len_ref, row_ref, bi_ref,
    pq, pk, pv, pout, pdo, sq, sk, sv, sout, sdo,
    dqp, dkp, dvp, dqr, dkr, dvr,
    kk, vv, lq, lout, ldo, tout, tdo, rq, rdo, rk, rv, rdel, dbuf,
    qa, doa, qT, doT, pt, own_pt, mh, mrun, lrun, delta, dqT, psc, dssc, bias,
    gpart, grecv, kept, ysb, yrb, zsb, zrb, dqrows, dkrows, dvrows, dqloc, dkvloc,
    kzs, kzr, kys, kyr, kcs, kcr, vzs, vzr, vys, vyr, vcs, vcr,
    as_, ar_, gcs, gcr, gys, gyr, gzs, gzr, bs_, br_, loc,
):
    c = lax.axis_index("ctx")
    r = lax.axis_index("resp")
    z = c // 4
    lane4 = c % 4
    core = c % 2
    ylo = lane4 // 2
    cpart = c + 1 - 2 * core
    ystep = 2 - 4 * ylo
    ypart = c + ystep

    def zpeer(d):
        return lax.rem(z + d, NZ) * 4 + lane4

    def rpeer(d):
        return lax.rem(r + d, nresp)

    def remote(src, dst, ss, rs, dev):
        return pltpu.make_async_remote_copy(
            src_ref=src, dst_ref=dst, send_sem=ss, recv_sem=rs, device_id=dev, device_id_type=MESH
        )

    def zoff(i):
        return jnp.where(i % 2 == 1, (i + 1) // 2, (NZ - i // 2) % NZ)

    def cols(ref, p, w):
        return ref.at[:, pl.ds(pl.multiple_of(p * w, 128), w)]

    def slots(ref, p):
        return ref.at[pl.ds(pl.multiple_of(p * 16, 16), 16), :]

    pairs = (
        lambda: (pk, kk.at[c]),
        lambda: (pv, vv.at[c]),
        lambda: (pq, lq),
        lambda: (pdo, ldo),
        lambda: (sdo, tdo),
        lambda: (sout, tout),
        lambda: (pout, lout),
        lambda: (cols(sq, r, QW), slots(rq, r)),
        lambda: (cols(sdo, r, QW), slots(rdo, r)),
        lambda: (cols(sk, r, HD), slots(rk, r)),
        lambda: (cols(sv, r, HD), slots(rv, r)),
        lambda: (dbuf.at[r], slots(rdel, r)),
        lambda: (dqloc, dqp),
        lambda: (dkvloc.at[0], dkp),
        lambda: (dkvloc.at[1], dvp),
        lambda: (slots(dqrows, r), cols(dqr, r, QW)),
        lambda: (slots(dkrows, r), cols(dkr, r, HD)),
        lambda: (slots(dvrows, r), cols(dvr, r, HD)),
    )

    def local(n):
        src, dst = pairs[n]()
        return pltpu.make_async_copy(src, dst, loc.at[n])

    for n in range(11):
        local(n).start()

    barrier = pltpu.get_barrier_semaphore()

    def greet(dev):
        pl.semaphore_signal(barrier, inc=1, device_id=dev, device_id_type=MESH)

    def greet_z(d, carry):
        greet((zpeer(d), r))
        return carry

    def greet_r(d, carry):
        greet((c, rpeer(d)))
        return carry

    lax.fori_loop(1, NZ, greet_z, 0)
    greet((cpart, r))
    greet((ypart, r))
    lax.fori_loop(1, nresp, greet_r, 0)
    pl.semaphore_wait(barrier, (NZ - 1) + (nresp - 1) + 2)

    def kz(d):
        return remote(kk.at[c], kk.at[c], kzs.at[d], kzr.at[NZ - d], (zpeer(d), r))

    def kz_wait(d):
        b = zpeer(d)
        remote(kk.at[b], kk.at[b], kzs.at[d], kzr.at[d], (b, r)).wait_recv()

    def ky(d):
        b = zpeer(d)
        return remote(kk.at[b], kk.at[b], kys.at[d], kyr.at[d], (ypart, r))

    def ky_wait(d):
        b = zpeer(d) + ystep
        remote(kk.at[b], kk.at[b], kys.at[d], kyr.at[d], (ypart, r)).wait_recv()

    def kc(d, far):
        b = zpeer(d) + far * ystep
        return remote(kk.at[b], kk.at[b], kcs.at[d, far], kcr.at[d, far], (cpart, r))

    def kc_wait(d, far):
        b = zpeer(d) + 1 - 2 * core + far * ystep
        remote(kk.at[b], kk.at[b], kcs.at[d, far], kcr.at[d, far], (cpart, r)).wait_recv()

    def pass_near(i):
        @pl.when(i < NZ)
        def _():
            d = zoff(i)
            kz_wait(d)
            ky(d).start()
            kc(d, 0).start()

    def pass_far(i):
        @pl.when(i < NZ)
        def _():
            d = zoff(i)
            ky_wait(d)
            kc(d, 1).start()

    def vy():
        return remote(vv.at[c], vv.at[c], vys.at[0], vyr.at[0], (ypart, r))

    def vy_wait():
        remote(vv.at[ypart], vv.at[ypart], vys.at[0], vyr.at[0], (ypart, r)).wait_recv()

    def vz(d, far):
        b = c + far * ystep
        return remote(vv.at[b], vv.at[b], vzs.at[d, far], vzr.at[NZ - d, far], (zpeer(d), r))

    def vz_wait(d, far):
        b = zpeer(d) + far * ystep
        remote(vv.at[b], vv.at[b], vzs.at[d, far], vzr.at[d, far], (zpeer(d), r)).wait_recv()

    def vc(d, far):
        b = zpeer(d) + far * ystep
        return remote(vv.at[b], vv.at[b], vcs.at[d, far], vcr.at[d, far], (cpart, r))

    def vc_wait(d, far):
        b = zpeer(d) + 1 - 2 * core + far * ystep
        remote(vv.at[b], vv.at[b], vcs.at[d, far], vcr.at[d, far], (cpart, r)).wait_recv()

    local(0).wait()
    ky(0).start()
    kc(0, 0).start()

    def send_keys(i, carry):
        kz(zoff(i)).start()
        return carry

    lax.fori_loop(1, NZ, send_keys, 0)
    local(1).wait()
    vy().start()
    vc(0, 0).start()

    lane = lax.broadcasted_iota(jnp.int32, (128, 128), 1)
    subl = lax.broadcasted_iota(jnp.int32, (128, 128), 0)
    diff = lane - subl
    my = bi_ref[c]

    def load_queries(q, do, base):
        for h in range(GROUP):
            sl = slice(h * HD, (h + 1) * HD)
            out = slice(base + h * BLK, base + (h + 1) * BLK)
            qh, dh = q[:, sl], do[:, sl]
            qa[out, :] = qh
            doa[out, :] = dh
            qT[:, out] = qh.T
            doT[:, out] = dh.T

    def place_delta(rows, base):
        rows_t = rows.T
        for h in range(GROUP):
            delta[:, base + h * BLK: base + (h + 1) * BLK] = rows_t[h:h + 1, :]

    local(2).wait()
    local(3).wait()
    load_queries(lq, ldo, 0)
    mrun[...] = jnp.full((8, 2 * QW), LOW, F32)
    lrun[...] = jnp.zeros((8, 2 * QW), F32)

    def near_first(i, carry):
        pass_near(i)
        return carry

    lax.fori_loop(1, LEAD + 1, near_first, 0)
    pass_far(0)

    def sources(p):
        return (cols(sq, p, QW), cols(sdo, p, QW), cols(sk, p, HD), cols(sv, p, HD), dbuf.at[p])

    landings = (rq, rdo, rk, rv, rdel)

    def exchange(d, which):
        p = rpeer(d)
        src = sources(p)
        return [
            remote(src[n], slots(landings[n], r), as_.at[n, d], ar_.at[n, nresp - d], (c, p))
            for n in which
        ]

    def exchange_in(d):
        p = rpeer(d)
        return [
            remote(slots(landings[n], p), slots(landings[n], p), as_.at[n, d], ar_.at[n, d], (c, p))
            for n in range(5)
        ]

    def send_rows(d, carry):
        for cp in exchange(d, range(4)):
            cp.start()
        return carry

    lax.fori_loop(1, nresp, send_rows, 0)
    local(4).wait()
    local(5).wait()
    lane16 = lax.broadcasted_iota(jnp.int32, (16, 128), 1)
    for g in range(nresp):
        acc = jnp.zeros((16, 128), F32)
        for h in range(GROUP):
            sl = slice((g * GROUP + h) * HD, (g * GROUP + h + 1) * HD)
            prod = tout[:, sl].astype(F32) * tdo[:, sl].astype(F32)
            acc = jnp.where(lane16 == h, jnp.sum(prod, axis=1, keepdims=True), acc)
        dbuf[g] = acc

    def send_delta(d, carry):
        exchange(d, (4,))[0].start()
        return carry

    lax.fori_loop(1, nresp, send_delta, 0)
    local(11).start()
    vy_wait()
    vc(0, 1).start()

    def merge(p3, m, mo, sl):
        mrun[:, sl] = m
        lrun[:, sl] = lrun[:, sl] * jnp.exp2((mo - m) * EXP_SCALE) + jnp.sum(p3, axis=0)

    def stats_chunk(i, base, masked):
        zc = lax.rem(z + zoff(i), NZ)
        if masked:
            for b in range(4):
                ahead = (bi_ref[zc * 4 + b] - my) * BLK
                bias[b * BLK:(b + 1) * BLK, :] = jnp.where(diff >= ahead, 0.0, NEG)
        for t in range(QW // QT):
            sl = slice(base + t * QT, base + (t + 1) * QT)
            for b in range(4):
                s = dot(kk[zc * 4 + b], qT[:, sl])
                if masked:
                    s = s + jnp.concatenate([bias[b * BLK:(b + 1) * BLK, :]] * (QT // BLK), axis=1)
                s3 = s.reshape(BLK // 8, 8, QT)
                mo = mrun[:, sl]
                m = jnp.maximum(mo, jnp.max(s3, axis=0))
                p3 = jnp.exp2((s3 - m[None]) * EXP_SCALE)
                prow = pl.ds(pl.multiple_of(i * CK + b * BLK, BLK), BLK)
                pt[prow, sl] = p3.reshape(BLK, QT).astype(BF16)
                mh[i * 4 + b, :, sl] = m
                merge(p3, m, mo, sl)

    def prompt_stats(i, carry):
        pass_near(i + LEAD + 1)
        pass_far(i + 1)
        d = zoff(i)

        @pl.when(i >= 1)
        def _():
            vz(d, 0).start()
            vz(d, 1).start()

        kc_wait(d, 0)
        kc_wait(d, 1)
        stats_chunk(i, 0, True)
        return carry

    lax.fori_loop(0, NZ, prompt_stats, 0)

    local(6).wait()
    acc = jnp.zeros((BLK, 128), F32)
    for h in range(GROUP):
        sl = slice(h * HD, (h + 1) * HD)
        prod = lout[:, sl].astype(F32) * ldo[:, sl].astype(F32)
        acc = jnp.where(lane == h, jnp.sum(prod, axis=1, keepdims=True), acc)
    place_delta(acc, 0)

    def wait_in(d, carry):
        for cp in exchange_in(d):
            cp.wait_recv()
        return carry

    lax.fori_loop(1, nresp, wait_in, 0)
    for n in range(7, 12):
        local(n).wait()
    load_queries(rq, rdo, QW)
    place_delta(rdel[...], QW)

    lane1 = lax.broadcasted_iota(jnp.int32, (1, 128), 1)
    startq = jnp.full((1, 128), DEAD, jnp.int32)
    cum = jnp.int32(0)
    for n in range(len_ref.shape[0]):
        count = jnp.where(row_ref[n] == c, len_ref[n], 0)
        startq = jnp.where((lane1 >= cum) & (lane1 < cum + count), cum, startq)
        cum = cum + count
    live = jnp.where(startq < DEAD, 1.0, 0.0)
    own_mask = (subl >= startq) & (diff >= 0)
    for h in range(GROUP):
        sl = slice(QW + h * BLK, QW + (h + 1) * BLK)
        s3 = jnp.where(own_mask, dot(rk[...], qT[:, sl]), NEG).reshape(BLK // 8, 8, BLK)
        mo = mrun[:, sl]
        m = jnp.maximum(mo, jnp.max(s3, axis=0))
        p3 = jnp.exp2((s3 - m[None]) * EXP_SCALE)
        own_pt[:, h * BLK:(h + 1) * BLK] = p3.reshape(BLK, BLK).astype(BF16)
        mh[4 * NZ, :, sl] = m
        merge(p3, m, mo, sl)

    def resp_stats(i, carry):
        d = zoff(i)

        @pl.when(i >= 1)
        def _():
            vz_wait(d, 0)
            vc(d, 0).start()
            vz_wait(d, 1)
            vc(d, 1).start()

        stats_chunk(i, QW, False)
        return carry

    lax.fori_loop(0, NZ, resp_stats, 0)

    peak = jnp.max(mrun[...], axis=0, keepdims=True)
    total = jnp.sum(lrun[...] * jnp.exp2((mrun[...] - peak) * EXP_SCALE), axis=0, keepdims=True)
    inv = jnp.where(total > 0.0, 1.0 / total, 0.0)
    inv = inv * jnp.concatenate([jnp.ones((1, QW), F32)] + [live] * GROUP, axis=1)
    for n in range(4 * NZ):
        mh[n] = jnp.exp2((mh[n] - peak) * EXP_SCALE) * inv
    own_f = jnp.exp2((mh[4 * NZ, :, QW:] - peak[:, QW:]) * EXP_SCALE) * inv[:, QW:]
    dqT[...] = jnp.zeros_like(dqT)

    def back(d, which):
        p = rpeer(d)
        dev = (c, p)
        e = nresp - d
        out = (
            lambda: remote(slots(dqrows, p), cols(dqr, r, QW), bs_.at[0, d], br_.at[0, e], dev),
            lambda: remote(slots(dkrows, p), cols(dkr, r, HD), bs_.at[1, d], br_.at[1, e], dev),
            lambda: remote(slots(dvrows, p), cols(dvr, r, HD), bs_.at[2, d], br_.at[2, e], dev),
        )
        return [out[n]() for n in which]

    def back_in(d):
        p = rpeer(d)
        dev = (c, p)
        return [
            remote(cols(dqr, p, QW), cols(dqr, p, QW), bs_.at[0, d], br_.at[0, d], dev),
            remote(cols(dkr, p, HD), cols(dkr, p, HD), bs_.at[1, d], br_.at[1, d], dev),
            remote(cols(dvr, p, HD), cols(dvr, p, HD), bs_.at[2, d], br_.at[2, d], dev),
        ]

    rkT = rk[...].T
    for h in range(GROUP):
        sl = slice(QW + h * BLK, QW + (h + 1) * BLK)
        hs = slice(h * BLK, (h + 1) * BLK)
        dp = dot(rv[...], doT[:, sl])
        p3 = own_pt[:, hs].astype(F32).reshape(BLK // 8, 8, BLK) * own_f[:, hs][None]
        p = p3.reshape(BLK, BLK)
        ds = (p * (dp - delta[:, sl])).astype(BF16)
        psc[0:BLK, sl] = p.astype(BF16)
        dssc[0:BLK, sl] = ds
        dqT[:, sl] += dot(rkT, ds)
    dvrows[...] = dot(psc[0:BLK, QW:], doa[QW:, :]).astype(BF16)
    dkrows[...] = (dot(dssc[0:BLK, QW:], qa[QW:, :]) * SCALE).astype(BF16)

    def send_back_kv(d, carry):
        for cp in back(d, (1, 2)):
            cp.start()
        return carry

    lax.fori_loop(1, nresp, send_back_kv, 0)
    local(16).start()
    local(17).start()

    def core_send(j):
        return remote(gpart.at[j, 1 - core], grecv.at[j], gcs.at[j], gcr.at[j], (cpart, r))

    def y_send(j):
        return remote(ysb.at[j], yrb.at[j], gys.at[j], gyr.at[j], (ypart, r))

    def z_send(j):
        d = zoff(NZ - 1 - j)
        return remote(zsb.at[j], zrb.at[NZ - d], gzs.at[d], gzr.at[NZ - d], (zpeer(d), r))

    def after_core(j):
        core_send(j).wait_recv()
        kept[j] = gpart[j, core, ylo] + grecv[j, ylo]
        ysb[j] = (gpart[j, core, 1 - ylo] + grecv[j, 1 - ylo]).astype(BF16)
        y_send(j).start()

    def after_y(j):
        y_send(j).wait_recv()
        zsb[j] = (kept[j] + yrb[j].astype(F32)).astype(BF16)
        z_send(j).start()

    def grads(j, carry):
        i = NZ - 1 - j
        d = zoff(i)
        zc = lax.rem(z + d, NZ)
        vc_wait(d, 0)
        vc_wait(d, 1)
        vc_rows = vv[pl.ds(zc * 4, 4)].reshape(CK, HD)
        kTc = kk[pl.ds(zc * 4, 4)].reshape(CK, HD).T
        prow = pl.ds(pl.multiple_of(i * CK, CK), CK)
        for t in range(2 * QW // QT):
            sl = slice(t * QT, (t + 1) * QT)
            dp = dot(vc_rows, doT[:, sl])
            f = mh[pl.ds(i * 4, 4), :, sl][:, None]
            p = (pt[prow, sl].astype(F32).reshape(4, BLK // 8, 8, QT) * f).reshape(CK, QT)
            ds = (p * (dp - delta[:, sl])).astype(BF16)
            psc[:, sl] = p.astype(BF16)
            dssc[:, sl] = ds
            dqT[:, sl] += dot(kTc, ds)
        dk = dot(dssc[...], qa[...])
        dv = dot(psc[...], doa[...])
        for b in range(4):
            gpart[j, b % 2, b // 2, 0] = dk[b * BLK:(b + 1) * BLK, :]
            gpart[j, b % 2, b // 2, 1] = dv[b * BLK:(b + 1) * BLK, :]
        core_send(j).start()

        @pl.when(j >= 1)
        def _():
            after_core(j - 1)

        @pl.when(j >= 2)
        def _():
            after_y(j - 2)

        return carry

    lax.fori_loop(0, NZ, grads, 0)

    for h in range(GROUP):
        dqrows[:, h * HD:(h + 1) * HD] = (dqT[:, QW + h * BLK:QW + (h + 1) * BLK].T * SCALE).astype(BF16)

    def send_back_q(d, carry):
        for cp in back(d, (0,)):
            cp.start()
        return carry

    lax.fori_loop(1, nresp, send_back_q, 0)
    local(15).start()

    after_core(NZ - 1)
    after_y(NZ - 2)
    for h in range(GROUP):
        dqloc[:, h * HD:(h + 1) * HD] = (dqT[:, h * BLK:(h + 1) * BLK].T * SCALE).astype(BF16)
    local(12).start()
    y_send(NZ - 1).wait_recv()
    kept[NZ - 1] = kept[NZ - 1] + yrb[NZ - 1].astype(F32)

    def drain_z(d, carry):
        kz(d).wait_send()
        vz(d, 0).wait_send()
        vz(d, 1).wait_send()
        return carry

    def drain_rest(d, carry):
        ky(d).wait_send()
        for far in range(2):
            kc(d, far).wait_send()
            vc(d, far).wait_send()
        return carry

    lax.fori_loop(1, NZ, drain_z, 0)
    lax.fori_loop(0, NZ, drain_rest, 0)
    vy().wait_send()

    def drain_exchange(d, carry):
        for cp in exchange(d, range(5)):
            cp.wait_send()
        return carry

    lax.fori_loop(1, nresp, drain_exchange, 0)

    def drain_parts(j, carry):
        core_send(j).wait_send()
        y_send(j).wait_send()
        return carry

    lax.fori_loop(0, NZ, drain_parts, 0)

    def drain_zparts(j, carry):
        z_send(j).wait_send()
        return carry

    def z_parts(d, carry):
        remote(zrb.at[d], zrb.at[d], gzs.at[d], gzr.at[d], (zpeer(d), r)).wait_recv()
        kept[NZ - 1] = kept[NZ - 1] + zrb[d].astype(F32)
        return carry

    lax.fori_loop(1, NZ, z_parts, 0)
    dkvloc[0] = (kept[NZ - 1, 0] * SCALE).astype(BF16)
    dkvloc[1] = kept[NZ - 1, 1].astype(BF16)
    local(13).start()
    local(14).start()
    lax.fori_loop(0, NZ - 1, drain_zparts, 0)

    def finish_back(d, carry):
        for cp in back(d, range(3)):
            cp.wait_send()
        for cp in back_in(d):
            cp.wait_recv()
        return carry

    lax.fori_loop(1, nresp, finish_back, 0)
    for n in range(12, 18):
        local(n).wait()


def settle(*refs):
    n = len(refs) // 2
    for src, dst in zip(refs[:n], refs[n:]):
        dst[...] = src[...]


def solution(mesh):
    nresp = mesh.shape["resp"]
    nctx = mesh.shape["ctx"]

    def body(
        prompt_q, prompt_k, prompt_v, prompt_out, prompt_dout,
        resp_q, resp_k, resp_v, resp_out, resp_dout,
        lengths, resp_row, block_index,
    ):
        shape = jax.ShapeDtypeStruct
        smem = pl.BlockSpec(memory_space=pltpu.SMEM)
        vmem = pl.BlockSpec(memory_space=pltpu.VMEM)
        dma = pltpu.SemaphoreType.DMA
        anywhere = pl.BlockSpec(memory_space=pl.ANY)
        parts = pl.pallas_call(
            functools.partial(kernel, nresp),
            out_shape=(
                shape(prompt_q.shape, BF16),
                shape(prompt_k.shape, BF16),
                shape(prompt_v.shape, BF16),
                shape(resp_q.shape, BF16),
                shape(resp_k.shape, BF16),
                shape(resp_v.shape, BF16),
            ),
            in_specs=[smem] * 3 + [anywhere] * 10,
            out_specs=(anywhere,) * 6,
            scratch_shapes=[
                pltpu.VMEM((nctx, BLK, HD), BF16),
                pltpu.VMEM((nctx, BLK, HD), BF16),
                pltpu.VMEM((BLK, QW), BF16),
                pltpu.VMEM((BLK, QW), BF16),
                pltpu.VMEM((BLK, QW), BF16),
                pltpu.VMEM(resp_out.shape, BF16),
                pltpu.VMEM(resp_out.shape, BF16),
                pltpu.VMEM((BLK, QW), BF16),
                pltpu.VMEM((BLK, QW), BF16),
                pltpu.VMEM((BLK, HD), BF16),
                pltpu.VMEM((BLK, HD), BF16),
                pltpu.VMEM((BLK, 128), F32),
                pltpu.VMEM((nresp, 16, 128), F32),
                pltpu.VMEM((2 * QW, HD), BF16),
                pltpu.VMEM((2 * QW, HD), BF16),
                pltpu.VMEM((HD, 2 * QW), BF16),
                pltpu.VMEM((HD, 2 * QW), BF16),
                pltpu.VMEM((nctx * BLK, 2 * QW), BF16),
                pltpu.VMEM((BLK, QW), BF16),
                pltpu.VMEM((nctx + 1, 8, 2 * QW), F32),
                pltpu.VMEM((8, 2 * QW), F32),
                pltpu.VMEM((8, 2 * QW), F32),
                pltpu.VMEM((1, 2 * QW), F32),
                pltpu.VMEM((HD, 2 * QW), F32),
                pltpu.VMEM((CK, 2 * QW), BF16),
                pltpu.VMEM((CK, 2 * QW), BF16),
                pltpu.VMEM((CK, BLK), F32),
                pltpu.VMEM((NZ, 2, 2, 2, BLK, HD), F32),
                pltpu.VMEM((NZ, 2, 2, BLK, HD), F32),
                pltpu.VMEM((NZ, 2, BLK, HD), F32),
                pltpu.VMEM((NZ, 2, BLK, HD), BF16),
                pltpu.VMEM((NZ, 2, BLK, HD), BF16),
                pltpu.VMEM((NZ, 2, BLK, HD), BF16),
                pltpu.VMEM((NZ, 2, BLK, HD), BF16),
                pltpu.VMEM((BLK, QW), BF16),
                pltpu.VMEM((BLK, HD), BF16),
                pltpu.VMEM((BLK, HD), BF16),
                pltpu.VMEM((BLK, QW), BF16),
                pltpu.VMEM((2, BLK, HD), BF16),
                dma((NZ,)), dma((NZ,)), dma((NZ,)), dma((NZ,)), dma((NZ, 2)), dma((NZ, 2)),
                dma((NZ, 2)), dma((NZ, 2)), dma((1,)), dma((1,)), dma((NZ, 2)), dma((NZ, 2)),
                dma((5, nresp)), dma((5, nresp)),
                dma((NZ,)), dma((NZ,)), dma((NZ,)), dma((NZ,)), dma((NZ,)), dma((NZ,)),
                dma((3, nresp)), dma((3, nresp)),
                dma((18,)),
            ],
            compiler_params=pltpu.CompilerParams(
                collective_id=0, has_side_effects=True, vmem_limit_bytes=60 * 1024 * 1024
            ),
            name="attn_bwd",
        )(
            lengths, resp_row, block_index,
            prompt_q, prompt_k, prompt_v, prompt_out, prompt_dout,
            resp_q, resp_k, resp_v, resp_out, resp_dout,
        )
        return pl.pallas_call(
            settle,
            out_shape=tuple(shape(part.shape, part.dtype) for part in parts),
            in_specs=[vmem] * 6,
            out_specs=(vmem,) * 6,
            compiler_params=pltpu.CompilerParams(vmem_limit_bytes=60 * 1024 * 1024),
            name="settle",
        )(*parts)

    heads, rows, whole = P("ctx", "resp"), P(("ctx", "resp"), None), P()
    return jax.shard_map(
        body,
        mesh=mesh,
        in_specs=(heads,) * 5 + (rows,) * 5 + (whole,) * 3,
        out_specs=(heads,) * 3 + (rows,) * 3,
        check_vma=False,
    )
```

time: 98.5 us -> 78.7 us (0.80)
  the two profiles are of different devices: /device:TPU:8 before, /device:TPU:1 now
where the time goes in v3:
time: 78.7 us; the launch traced here: 77.2 us
  Pallas kernels  76.6 us (97%)
    pallas_call x1, Pallas kernels, body(): pl.pallas_call(functools.partial(kernel, nresp), out_shape=(shape(prompt_...  74.7 us
    pallas_call x1, Pallas kernels, body(): pl.pallas_call(settle, out_shape=tuple((shape(part.shape, part.dtype) for...  1.89 us

profile of v3, /device:TPU:1, one launch (start us, length us, event | category | flops | bytes accessed | tf_op | source)
XLA Modules:
  0.0 77.2 jit_solution(1906784383249980227)
XLA Ops:
  0.6 74.7 %attn_bwd.1 = (bf16[128,1024]{1,0:T(8,128)(2,1)}, bf16[128,128]{1,0:T(8,128)(2,1)}, bf16[128,128]{1,0:T(8,128)(2,1)}, bf16[16,8192]{1,0:T(8,128)(2,1)}, bf16[16,...) custom-call(s32[16]{0:T(128)} %len_ref.1, s32[16]{0:T(128)} %row_ref.1, s32[32]{0:T(128)} %bi_ref.1, bf16[128,1024]{1,0:T(8,128)(2,1)} %pq.1, ...), custom_call_target="tpu_custom_call" | custom-call | tf_op jit(solution)/shard_map/attn_bwd/pallas_call | solution.py:574
  75.3 1.9 %settle.1 = (bf16[128,1024]{1,0:T(8,128)(2,1)}, bf16[128,128]{1,0:T(8,128)(2,1)}, bf16[128,128]{1,0:T(8,128)(2,1)}, bf16[16,8192]{1,0:T(8,128)(2,1)}, bf16[16,10...) custom-call(bf16[128,1024]{1,0:T(8,128)(2,1)} %get-tuple-element.12.refs_0_, bf16[128,128]{1,0:T(8,128)(2,1)} %get-tuple-element.13.refs_1_, ...), custom_call_target="tpu_custom_call" | custom-call | tf_op jit(solution)/shard_map/settle/pallas_call | solution.py:642

commit v4 on v3

--- a/solution.py
+++ b/solution.py
@@ -13,7 +13,6 @@
 GROUP = 8
 BLK = 128
 NZ = 8
-LEAD = 3
 QW = GROUP * BLK
 CK = 4 * BLK
 QT = 512
@@ -116,78 +115,109 @@
     lax.fori_loop(1, nresp, greet_r, 0)
     pl.semaphore_wait(barrier, (NZ - 1) + (nresp - 1) + 2)
 
-    def kz(d):
-        return remote(kk.at[c], kk.at[c], kzs.at[d], kzr.at[NZ - d], (zpeer(d), r))
-
-    def kz_wait(d):
-        b = zpeer(d)
-        remote(kk.at[b], kk.at[b], kzs.at[d], kzr.at[d], (b, r)).wait_recv()
-
-    def ky(d):
-        b = zpeer(d)
-        return remote(kk.at[b], kk.at[b], kys.at[d], kyr.at[d], (ypart, r))
-
-    def ky_wait(d):
-        b = zpeer(d) + ystep
-        remote(kk.at[b], kk.at[b], kys.at[d], kyr.at[d], (ypart, r)).wait_recv()
-
-    def kc(d, far):
+    ksems = (kk, kzs, kzr, kys, kyr, kcs, kcr)
+    vsems = (vv, vzs, vzr, vys, vyr, vcs, vcr)
+
+    def y_swap(sems):
+        ref, zs, zr, ys, yr, cs, cr = sems
+        return remote(ref.at[c], ref.at[c], ys.at[0], yr.at[0], (ypart, r))
+
+    def y_wait(sems):
+        ref, zs, zr, ys, yr, cs, cr = sems
+        remote(ref.at[ypart], ref.at[ypart], ys.at[0], yr.at[0], (ypart, r)).wait_recv()
+
+    def hop(sems, d, e, far, to):
+        ref, zs, zr, ys, yr, cs, cr = sems
         b = zpeer(d) + far * ystep
-        return remote(kk.at[b], kk.at[b], kcs.at[d, far], kcr.at[d, far], (cpart, r))
-
-    def kc_wait(d, far):
+        return remote(ref.at[b], ref.at[b], zs.at[e, far], zr.at[e, far], (to, r))
+
+    def hop_wait(sems, d, far):
+        ref, zs, zr, ys, yr, cs, cr = sems
+        b = zpeer(d) + far * ystep
+        remote(ref.at[b], ref.at[b], zs.at[d, far], zr.at[d, far], (zpeer(1), r)).wait_recv()
+
+    def share(sems, d, far):
+        ref, zs, zr, ys, yr, cs, cr = sems
+        b = zpeer(d) + far * ystep
+        return remote(ref.at[b], ref.at[b], cs.at[d, far], cr.at[d, far], (cpart, r))
+
+    def share_wait(sems, d, far):
+        ref, zs, zr, ys, yr, cs, cr = sems
         b = zpeer(d) + 1 - 2 * core + far * ystep
-        remote(kk.at[b], kk.at[b], kcs.at[d, far], kcr.at[d, far], (cpart, r)).wait_recv()
-
-    def pass_near(i):
-        @pl.when(i < NZ)
-        def _():
-            d = zoff(i)
-            kz_wait(d)
-            ky(d).start()
-            kc(d, 0).start()
-
-    def pass_far(i):
-        @pl.when(i < NZ)
-        def _():
-            d = zoff(i)
-            ky_wait(d)
-            kc(d, 1).start()
-
-    def vy():
-        return remote(vv.at[c], vv.at[c], vys.at[0], vyr.at[0], (ypart, r))
-
-    def vy_wait():
-        remote(vv.at[ypart], vv.at[ypart], vys.at[0], vyr.at[0], (ypart, r)).wait_recv()
-
-    def vz(d, far):
-        b = c + far * ystep
-        return remote(vv.at[b], vv.at[b], vzs.at[d, far], vzr.at[NZ - d, far], (zpeer(d), r))
-
-    def vz_wait(d, far):
-        b = zpeer(d) + far * ystep
-        remote(vv.at[b], vv.at[b], vzs.at[d, far], vzr.at[d, far], (zpeer(d), r)).wait_recv()
-
-    def vc(d, far):
-        b = zpeer(d) + far * ystep
-        return remote(vv.at[b], vv.at[b], vcs.at[d, far], vcr.at[d, far], (cpart, r))
-
-    def vc_wait(d, far):
-        b = zpeer(d) + 1 - 2 * core + far * ystep
-        remote(vv.at[b], vv.at[b], vcs.at[d, far], vcr.at[d, far], (cpart, r)).wait_recv()
+        remote(ref.at[b], ref.at[b], cs.at[d, far], cr.at[d, far], (cpart, r)).wait_recv()
+
+    def begin(sems, far):
+        hop(sems, 0, 1, far, zpeer(NZ - 1)).start()
+        hop(sems, 0, NZ - 1, far, zpeer(1)).start()
+        share(sems, 0, far).start()
+
+    def relay(sems, i):
+        d = zoff(i)
+        odd = i % 2 == 1
+        e = jnp.where(odd, d + 1, d - 1)
+        to = jnp.where(odd, zpeer(NZ - 1), zpeer(1))
+        for far in range(2):
+            hop_wait(sems, d, far)
+
+            @pl.when((i <= NZ - 4) | (i == NZ - 3 + far))
+            def _():
+                hop(sems, d, e, far, to).start()
+
+            share(sems, d, far).start()
+
+    def drain_gather(sems):
+        ref, zs, zr, ys, yr, cs, cr = sems
+
+        def drain_hops(e, carry):
+            for far in range(2):
+                hop(sems, 0, e, far, zpeer(1)).wait_send()
+            return carry
+
+        def drain_shares(d, carry):
+            for far in range(2):
+                share(sems, d, far).wait_send()
+            return carry
+
+        lax.fori_loop(1, NZ, drain_hops, 0)
+        lax.fori_loop(0, NZ, drain_shares, 0)
+        y_swap(sems).wait_send()
+
+    def sources(p):
+        return (cols(sq, p, QW), cols(sdo, p, QW), cols(sk, p, HD), cols(sv, p, HD), dbuf.at[p])
+
+    landings = (rq, rdo, rk, rv, rdel)
+
+    def exchange(d, which):
+        p = rpeer(d)
+        src = sources(p)
+        return [
+            remote(src[n], slots(landings[n], r), as_.at[n, d], ar_.at[n, nresp - d], (c, p))
+            for n in which
+        ]
+
+    def exchange_in(d):
+        p = rpeer(d)
+        return [
+            remote(slots(landings[n], p), slots(landings[n], p), as_.at[n, d], ar_.at[n, d], (c, p))
+            for n in range(5)
+        ]
+
+    def send_rows(d, carry):
+        for cp in exchange(d, range(4)):
+            cp.start()
+        return carry
 
     local(0).wait()
-    ky(0).start()
-    kc(0, 0).start()
-
-    def send_keys(i, carry):
-        kz(zoff(i)).start()
-        return carry
-
-    lax.fori_loop(1, NZ, send_keys, 0)
+    y_swap(ksems).start()
+    begin(ksems, 0)
     local(1).wait()
-    vy().start()
-    vc(0, 0).start()
+    y_swap(vsems).start()
+    y_wait(ksems)
+    begin(ksems, 1)
+    begin(vsems, 0)
+    y_wait(vsems)
+    begin(vsems, 1)
+    lax.fori_loop(1, nresp, send_rows, 0)
 
     lane = lax.broadcasted_iota(jnp.int32, (128, 128), 1)
     subl = lax.broadcasted_iota(jnp.int32, (128, 128), 0)
@@ -215,39 +245,7 @@
     mrun[...] = jnp.full((8, 2 * QW), LOW, F32)
     lrun[...] = jnp.zeros((8, 2 * QW), F32)
 
-    def near_first(i, carry):
-        pass_near(i)
-        return carry
-
-    lax.fori_loop(1, LEAD + 1, near_first, 0)
-    pass_far(0)
-
-    def sources(p):
-        return (cols(sq, p, QW), cols(sdo, p, QW), cols(sk, p, HD), cols(sv, p, HD), dbuf.at[p])
-
-    landings = (rq, rdo, rk, rv, rdel)
-
-    def exchange(d, which):
-        p = rpeer(d)
-        src = sources(p)
-        return [
-            remote(src[n], slots(landings[n], r), as_.at[n, d], ar_.at[n, nresp - d], (c, p))
-            for n in which
-        ]
-
-    def exchange_in(d):
-        p = rpeer(d)
-        return [
-            remote(slots(landings[n], p), slots(landings[n], p), as_.at[n, d], ar_.at[n, d], (c, p))
-            for n in range(5)
-        ]
-
-    def send_rows(d, carry):
-        for cp in exchange(d, range(4)):
-            cp.start()
-        return carry
-
-    lax.fori_loop(1, nresp, send_rows, 0)
+    relay(ksems, 1)
     local(4).wait()
     local(5).wait()
     lane16 = lax.broadcasted_iota(jnp.int32, (16, 128), 1)
@@ -265,8 +263,6 @@
 
     lax.fori_loop(1, nresp, send_delta, 0)
     local(11).start()
-    vy_wait()
-    vc(0, 1).start()
 
     def merge(p3, m, mo, sl):
         mrun[:, sl] = m
@@ -294,17 +290,17 @@
                 merge(p3, m, mo, sl)
 
     def prompt_stats(i, carry):
-        pass_near(i + LEAD + 1)
-        pass_far(i + 1)
+        @pl.when(i < NZ - 2)
+        def _():
+            relay(ksems, i + 2)
+
+        @pl.when(i < NZ - 1)
+        def _():
+            relay(vsems, i + 1)
+
         d = zoff(i)
-
-        @pl.when(i >= 1)
-        def _():
-            vz(d, 0).start()
-            vz(d, 1).start()
-
-        kc_wait(d, 0)
-        kc_wait(d, 1)
+        share_wait(ksems, d, 0)
+        share_wait(ksems, d, 1)
         stats_chunk(i, 0, True)
         return carry
 
@@ -349,15 +345,6 @@
         merge(p3, m, mo, sl)
 
     def resp_stats(i, carry):
-        d = zoff(i)
-
-        @pl.when(i >= 1)
-        def _():
-            vz_wait(d, 0)
-            vc(d, 0).start()
-            vz_wait(d, 1)
-            vc(d, 1).start()
-
         stats_chunk(i, QW, False)
         return carry
 
@@ -440,8 +427,8 @@
         i = NZ - 1 - j
         d = zoff(i)
         zc = lax.rem(z + d, NZ)
-        vc_wait(d, 0)
-        vc_wait(d, 1)
+        share_wait(vsems, d, 0)
+        share_wait(vsems, d, 1)
         vc_rows = vv[pl.ds(zc * 4, 4)].reshape(CK, HD)
         kTc = kk[pl.ds(zc * 4, 4)].reshape(CK, HD).T
         prow = pl.ds(pl.multiple_of(i * CK, CK), CK)
@@ -492,22 +479,8 @@
     y_send(NZ - 1).wait_recv()
     kept[NZ - 1] = kept[NZ - 1] + yrb[NZ - 1].astype(F32)
 
-    def drain_z(d, carry):
-        kz(d).wait_send()
-        vz(d, 0).wait_send()
-        vz(d, 1).wait_send()
-        return carry
-
-    def drain_rest(d, carry):
-        ky(d).wait_send()
-        for far in range(2):
-            kc(d, far).wait_send()
-            vc(d, far).wait_send()
-        return carry
-
-    lax.fori_loop(1, NZ, drain_z, 0)
-    lax.fori_loop(0, NZ, drain_rest, 0)
-    vy().wait_send()
+    drain_gather(ksems)
+    drain_gather(vsems)
 
     def drain_exchange(d, carry):
         for cp in exchange(d, range(5)):
@@ -623,7 +596,7 @@
                 pltpu.VMEM((BLK, HD), BF16),
                 pltpu.VMEM((BLK, QW), BF16),
                 pltpu.VMEM((2, BLK, HD), BF16),
-                dma((NZ,)), dma((NZ,)), dma((NZ,)), dma((NZ,)), dma((NZ, 2)), dma((NZ, 2)),
+                dma((NZ, 2)), dma((NZ, 2)), dma((1,)), dma((1,)), dma((NZ, 2)), dma((NZ, 2)),
                 dma((NZ, 2)), dma((NZ, 2)), dma((1,)), dma((1,)), dma((NZ, 2)), dma((NZ, 2)),
                 dma((5, nresp)), dma((5, nresp)),
                 dma((NZ,)), dma((NZ,)), dma((NZ,)), dma((NZ,)), dma((NZ,)), dma((NZ,)),

time: 78.7 us -> 76.3 us (0.970); the launches traced: 77.2 us -> 76.2 us
  Pallas kernels: 76.6 us -> 75.6 us
    pallas_call x1, Pallas kernels: 74.7 us -> 73.7 us  [body(): pl.pallas_call(functools.partial(kernel, nresp), out_shape=(shape(prompt_...]
where the time goes in v4:
time: 76.3 us; the launch traced here: 76.2 us
  Pallas kernels  75.6 us (99%)
    pallas_call x1, Pallas kernels, body(): pl.pallas_call(functools.partial(kernel, nresp), out_shape=(shape(prompt_...  73.7 us
    pallas_call x1, Pallas kernels, body(): pl.pallas_call(settle, out_shape=tuple((shape(part.shape, part.dtype) for...  1.89 us

profile of v4, /device:TPU:1, one launch (start us, length us, event | category | flops | bytes accessed | tf_op | source)
XLA Modules:
  0.0 76.2 jit_solution(1747927974940063157)
XLA Ops:
  0.6 73.7 %attn_bwd.1 = (bf16[128,1024]{1,0:T(8,128)(2,1)}, bf16[128,128]{1,0:T(8,128)(2,1)}, bf16[128,128]{1,0:T(8,128)(2,1)}, bf16[16,8192]{1,0:T(8,128)(2,1)}, bf16[16,...) custom-call(s32[16]{0:T(128)} %len_ref.1, s32[16]{0:T(128)} %row_ref.1, s32[32]{0:T(128)} %bi_ref.1, bf16[128,1024]{1,0:T(8,128)(2,1)} %pq.1, ...), custom_call_target="tpu_custom_call" | custom-call | tf_op jit(solution)/shard_map/attn_bwd/pallas_call | solution.py:547
  74.3 1.9 %settle.1 = (bf16[128,1024]{1,0:T(8,128)(2,1)}, bf16[128,128]{1,0:T(8,128)(2,1)}, bf16[128,128]{1,0:T(8,128)(2,1)}, bf16[16,8192]{1,0:T(8,128)(2,1)}, bf16[16,10...) custom-call(bf16[128,1024]{1,0:T(8,128)(2,1)} %get-tuple-element.12.refs_0_, bf16[128,128]{1,0:T(8,128)(2,1)} %get-tuple-element.13.refs_1_, ...), custom_call_target="tpu_custom_call" | custom-call | tf_op jit(solution)/shard_map/settle/pallas_call | solution.py:615

commit v5 on v4

--- a/solution.py
+++ b/solution.py
@@ -13,6 +13,7 @@
 GROUP = 8
 BLK = 128
 NZ = 8
+LEAD = 3
 QW = GROUP * BLK
 CK = 4 * BLK
 QT = 512
@@ -118,18 +119,21 @@
     ksems = (kk, kzs, kzr, kys, kyr, kcs, kcr)
     vsems = (vv, vzs, vzr, vys, vyr, vcs, vcr)
 
-    def y_swap(sems):
+    def swap(sems, d):
         ref, zs, zr, ys, yr, cs, cr = sems
-        return remote(ref.at[c], ref.at[c], ys.at[0], yr.at[0], (ypart, r))
-
-    def y_wait(sems):
+        b = zpeer(d)
+        return remote(ref.at[b], ref.at[b], ys.at[d], yr.at[d], (ypart, r))
+
+    def swap_wait(sems, d):
         ref, zs, zr, ys, yr, cs, cr = sems
-        remote(ref.at[ypart], ref.at[ypart], ys.at[0], yr.at[0], (ypart, r)).wait_recv()
-
-    def hop(sems, d, e, far, to):
+        b = zpeer(d) + ystep
+        remote(ref.at[b], ref.at[b], ys.at[d], yr.at[d], (ypart, r)).wait_recv()
+
+    def hop(sems, d, e, far):
         ref, zs, zr, ys, yr, cs, cr = sems
         b = zpeer(d) + far * ystep
-        return remote(ref.at[b], ref.at[b], zs.at[e, far], zr.at[e, far], (to, r))
+        to = (zpeer(lax.rem(d - e + NZ, NZ)), r)
+        return remote(ref.at[b], ref.at[b], zs.at[e, far], zr.at[e, far], to)
 
     def hop_wait(sems, d, far):
         ref, zs, zr, ys, yr, cs, cr = sems
@@ -146,41 +150,66 @@
         b = zpeer(d) + 1 - 2 * core + far * ystep
         remote(ref.at[b], ref.at[b], cs.at[d, far], cr.at[d, far], (cpart, r)).wait_recv()
 
-    def begin(sems, far):
-        hop(sems, 0, 1, far, zpeer(NZ - 1)).start()
-        hop(sems, 0, NZ - 1, far, zpeer(1)).start()
-        share(sems, 0, far).start()
-
-    def relay(sems, i):
+    def send_keys(i, carry):
+        hop(ksems, 0, zoff(i), 0).start()
+        return carry
+
+    def key_near(i):
+        @pl.when(i < NZ)
+        def _():
+            d = zoff(i)
+            hop_wait(ksems, d, 0)
+            swap(ksems, d).start()
+            share(ksems, d, 0).start()
+
+    def key_far(i):
+        @pl.when(i < NZ)
+        def _():
+            d = zoff(i)
+            swap_wait(ksems, d)
+            share(ksems, d, 1).start()
+
+    def send_values(far):
+        for e in (1, NZ - 1, 2, NZ - 2):
+            hop(vsems, 0, e, far).start()
+        share(vsems, 0, far).start()
+
+    def value_step(i):
         d = zoff(i)
-        odd = i % 2 == 1
-        e = jnp.where(odd, d + 1, d - 1)
-        to = jnp.where(odd, zpeer(NZ - 1), zpeer(1))
         for far in range(2):
-            hop_wait(sems, d, far)
-
-            @pl.when((i <= NZ - 4) | (i == NZ - 3 + far))
+            hop_wait(vsems, d, far)
+
+            @pl.when(i == 3)
             def _():
-                hop(sems, d, e, far, to).start()
-
-            share(sems, d, far).start()
-
-    def drain_gather(sems):
-        ref, zs, zr, ys, yr, cs, cr = sems
-
+                hop(vsems, 2, 3, far).start()
+
+            @pl.when(i == 4)
+            def _():
+                hop(vsems, NZ - 2, NZ - 3, far).start()
+
+            @pl.when(i == 3 + far)
+            def _():
+                hop(vsems, d, 4, far).start()
+
+            share(vsems, d, far).start()
+
+    def drain_gather():
         def drain_hops(e, carry):
+            hop(ksems, 0, e, 0).wait_send()
             for far in range(2):
-                hop(sems, 0, e, far, zpeer(1)).wait_send()
+                hop(vsems, 0, e, far).wait_send()
             return carry
 
         def drain_shares(d, carry):
+            swap(ksems, d).wait_send()
             for far in range(2):
-                share(sems, d, far).wait_send()
+                share(ksems, d, far).wait_send()
+                share(vsems, d, far).wait_send()
             return carry
 
         lax.fori_loop(1, NZ, drain_hops, 0)
         lax.fori_loop(0, NZ, drain_shares, 0)
-        y_swap(sems).wait_send()
+        swap(vsems, 0).wait_send()
 
     def sources(p):
         return (cols(sq, p, QW), cols(sdo, p, QW), cols(sk, p, HD), cols(sv, p, HD), dbuf.at[p])
@@ -202,22 +231,18 @@
             for n in range(5)
         ]
 
-    def send_rows(d, carry):
-        for cp in exchange(d, range(4)):
+    def send_rows(n, carry):
+        for cp in exchange(n, range(4)):
             cp.start()
         return carry
 
     local(0).wait()
-    y_swap(ksems).start()
-    begin(ksems, 0)
+    swap(ksems, 0).start()
+    share(ksems, 0, 0).start()
+    lax.fori_loop(1, NZ, send_keys, 0)
     local(1).wait()
-    y_swap(vsems).start()
-    y_wait(ksems)
-    begin(ksems, 1)
-    begin(vsems, 0)
-    y_wait(vsems)
-    begin(vsems, 1)
-    lax.fori_loop(1, nresp, send_rows, 0)
+    swap(vsems, 0).start()
+    lax.fori_loop(1, nresp // 2, lambda n, carry: send_rows(2 * n, carry), 0)
 
     lane = lax.broadcasted_iota(jnp.int32, (128, 128), 1)
     subl = lax.broadcasted_iota(jnp.int32, (128, 128), 0)
@@ -245,7 +270,16 @@
     mrun[...] = jnp.full((8, 2 * QW), LOW, F32)
     lrun[...] = jnp.zeros((8, 2 * QW), F32)
 
-    relay(ksems, 1)
+    def near_first(i, carry):
+        key_near(i)
+        return carry
+
+    lax.fori_loop(1, LEAD + 1, near_first, 0)
+    key_far(0)
+    lax.fori_loop(0, nresp // 2, lambda n, carry: send_rows(2 * n + 1, carry), 0)
+    send_values(0)
+    swap_wait(vsems, 0)
+    send_values(1)
     local(4).wait()
     local(5).wait()
     lane16 = lax.broadcasted_iota(jnp.int32, (16, 128), 1)
@@ -290,13 +324,12 @@
                 merge(p3, m, mo, sl)
 
     def prompt_stats(i, carry):
-        @pl.when(i < NZ - 2)
+        key_near(i + LEAD + 1)
+        key_far(i + 1)
+
+        @pl.when(i >= NZ - 4)
         def _():
-            relay(ksems, i + 2)
-
-        @pl.when(i < NZ - 1)
-        def _():
-            relay(vsems, i + 1)
+            value_step(i - (NZ - 5))
 
         d = zoff(i)
         share_wait(ksems, d, 0)
@@ -345,6 +378,10 @@
         merge(p3, m, mo, sl)
 
     def resp_stats(i, carry):
+        @pl.when(i < NZ - 5)
+        def _():
+            value_step(i + NZ - 3)
+
         stats_chunk(i, QW, False)
         return carry
 
@@ -441,6 +478,11 @@
             psc[:, sl] = p.astype(BF16)
             dssc[:, sl] = ds
             dqT[:, sl] += dot(kTc, ds)
+            if t == 1:
+                @pl.when(j >= 1)
+                def _():
+                    after_core(j - 1)
+
         dk = dot(dssc[...], qa[...])
         dv = dot(psc[...], doa[...])
         for b in range(4):
@@ -450,11 +492,7 @@
 
         @pl.when(j >= 1)
         def _():
-            after_core(j - 1)
-
-        @pl.when(j >= 2)
-        def _():
-            after_y(j - 2)
+            after_y(j - 1)
 
         return carry
 
@@ -472,15 +510,13 @@
     local(15).start()
 
     after_core(NZ - 1)
-    after_y(NZ - 2)
     for h in range(GROUP):
         dqloc[:, h * HD:(h + 1) * HD] = (dqT[:, h * BLK:(h + 1) * BLK].T * SCALE).astype(BF16)
     local(12).start()
     y_send(NZ - 1).wait_recv()
     kept[NZ - 1] = kept[NZ - 1] + yrb[NZ - 1].astype(F32)
 
-    drain_gather(ksems)
-    drain_gather(vsems)
+    drain_gather()
 
     def drain_exchange(d, carry):
         for cp in exchange(d, range(5)):
@@ -596,8 +632,8 @@
                 pltpu.VMEM((BLK, HD), BF16),
                 pltpu.VMEM((BLK, QW), BF16),
                 pltpu.VMEM((2, BLK, HD), BF16),
-                dma((NZ, 2)), dma((NZ, 2)), dma((1,)), dma((1,)), dma((NZ, 2)), dma((NZ, 2)),
-                dma((NZ, 2)), dma((NZ, 2)), dma((1,)), dma((1,)), dma((NZ, 2)), dma((NZ, 2)),
+                dma((NZ, 2)), dma((NZ, 2)), dma((NZ,)), dma((NZ,)), dma((NZ, 2)), dma((NZ, 2)),
+                dma((NZ, 2)), dma((NZ, 2)), dma((NZ,)), dma((NZ,)), dma((NZ, 2)), dma((NZ, 2)),
                 dma((5, nresp)), dma((5, nresp)),
                 dma((NZ,)), dma((NZ,)), dma((NZ,)), dma((NZ,)), dma((NZ,)), dma((NZ,)),
                 dma((3, nresp)), dma((3, nresp)),

time: 76.3 us -> 85.1 us (1.12)
  Pallas kernels: 75.6 us -> 84.4 us
    pallas_call x1, Pallas kernels: 73.7 us -> 82.5 us  [body(): pl.pallas_call(functools.partial(kernel, nresp), out_shape=(shape(prompt_...]
where the time goes in v5:
time: 85.1 us; the launch traced here: 85 us
  Pallas kernels  84.4 us (99%)
    pallas_call x1, Pallas kernels, body(): pl.pallas_call(functools.partial(kernel, nresp), out_shape=(shape(prompt_...  82.5 us
    pallas_call x1, Pallas kernels, body(): pl.pallas_call(settle, out_shape=tuple((shape(part.shape, part.dtype) for...  1.89 us

profile of v5, /device:TPU:1, one launch (start us, length us, event | category | flops | bytes accessed | tf_op | source)
XLA Modules:
  0.0 85.0 jit_solution(14363869917117226256)
XLA Ops:
  0.6 82.5 %attn_bwd.1 = (bf16[128,1024]{1,0:T(8,128)(2,1)}, bf16[128,128]{1,0:T(8,128)(2,1)}, bf16[128,128]{1,0:T(8,128)(2,1)}, bf16[16,8192]{1,0:T(8,128)(2,1)}, bf16[16,...) custom-call(s32[16]{0:T(128)} %len_ref.1, s32[16]{0:T(128)} %row_ref.1, s32[32]{0:T(128)} %bi_ref.1, bf16[128,1024]{1,0:T(8,128)(2,1)} %pq.1, ...), custom_call_target="tpu_custom_call" | custom-call | tf_op jit(solution)/shard_map/attn_bwd/pallas_call | solution.py:583
  83.1 1.9 %settle.1 = (bf16[128,1024]{1,0:T(8,128)(2,1)}, bf16[128,128]{1,0:T(8,128)(2,1)}, bf16[128,128]{1,0:T(8,128)(2,1)}, bf16[16,8192]{1,0:T(8,128)(2,1)}, bf16[16,10...) custom-call(bf16[128,1024]{1,0:T(8,128)(2,1)} %get-tuple-element.12.refs_0_, bf16[128,128]{1,0:T(8,128)(2,1)} %get-tuple-element.13.refs_1_, ...), custom_call_target="tpu_custom_call" | custom-call | tf_op jit(solution)/shard_map/settle/pallas_call | solution.py:651

commit v6 on v4

--- a/solution.py
+++ b/solution.py
@@ -118,18 +118,19 @@
     ksems = (kk, kzs, kzr, kys, kyr, kcs, kcr)
     vsems = (vv, vzs, vzr, vys, vyr, vcs, vcr)
 
-    def y_swap(sems):
+    def swap(sems):
         ref, zs, zr, ys, yr, cs, cr = sems
         return remote(ref.at[c], ref.at[c], ys.at[0], yr.at[0], (ypart, r))
 
-    def y_wait(sems):
+    def swap_wait(sems):
         ref, zs, zr, ys, yr, cs, cr = sems
         remote(ref.at[ypart], ref.at[ypart], ys.at[0], yr.at[0], (ypart, r)).wait_recv()
 
-    def hop(sems, d, e, far, to):
+    def hop(sems, d, e, far):
         ref, zs, zr, ys, yr, cs, cr = sems
         b = zpeer(d) + far * ystep
-        return remote(ref.at[b], ref.at[b], zs.at[e, far], zr.at[e, far], (to, r))
+        to = (zpeer(lax.rem(d - e + NZ, NZ)), r)
+        return remote(ref.at[b], ref.at[b], zs.at[e, far], zr.at[e, far], to)
 
     def hop_wait(sems, d, far):
         ref, zs, zr, ys, yr, cs, cr = sems
@@ -147,30 +148,28 @@
         remote(ref.at[b], ref.at[b], cs.at[d, far], cr.at[d, far], (cpart, r)).wait_recv()
 
     def begin(sems, far):
-        hop(sems, 0, 1, far, zpeer(NZ - 1)).start()
-        hop(sems, 0, NZ - 1, far, zpeer(1)).start()
+        for e in (1, NZ - 1, 2, NZ - 2):
+            hop(sems, 0, e, far).start()
         share(sems, 0, far).start()
 
-    def relay(sems, i):
+    def arrived(sems, i):
         d = zoff(i)
-        odd = i % 2 == 1
-        e = jnp.where(odd, d + 1, d - 1)
-        to = jnp.where(odd, zpeer(NZ - 1), zpeer(1))
         for far in range(2):
             hop_wait(sems, d, far)
-
-            @pl.when((i <= NZ - 4) | (i == NZ - 3 + far))
-            def _():
-                hop(sems, d, e, far, to).start()
-
             share(sems, d, far).start()
 
+    def relay(sems, d, e):
+        for far in range(2):
+            hop_wait(sems, d, far)
+            hop(sems, d, e, far).start()
+        hop(sems, d, NZ // 2, d // (NZ // 2)).start()
+        for far in range(2):
+            share(sems, d, far).start()
+
     def drain_gather(sems):
-        ref, zs, zr, ys, yr, cs, cr = sems
-
         def drain_hops(e, carry):
             for far in range(2):
-                hop(sems, 0, e, far, zpeer(1)).wait_send()
+                hop(sems, 0, e, far).wait_send()
             return carry
 
         def drain_shares(d, carry):
@@ -180,7 +179,7 @@
 
         lax.fori_loop(1, NZ, drain_hops, 0)
         lax.fori_loop(0, NZ, drain_shares, 0)
-        y_swap(sems).wait_send()
+        swap(sems).wait_send()
 
     def sources(p):
         return (cols(sq, p, QW), cols(sdo, p, QW), cols(sk, p, HD), cols(sv, p, HD), dbuf.at[p])
@@ -202,22 +201,19 @@
             for n in range(5)
         ]
 
-    def send_rows(d, carry):
-        for cp in exchange(d, range(4)):
+    def send_rows(n, carry):
+        for cp in exchange(n, range(4)):
             cp.start()
         return carry
 
     local(0).wait()
-    y_swap(ksems).start()
+    swap(ksems).start()
     begin(ksems, 0)
     local(1).wait()
-    y_swap(vsems).start()
-    y_wait(ksems)
+    swap(vsems).start()
+    lax.fori_loop(1, nresp, send_rows, 0)
+    swap_wait(ksems)
     begin(ksems, 1)
-    begin(vsems, 0)
-    y_wait(vsems)
-    begin(vsems, 1)
-    lax.fori_loop(1, nresp, send_rows, 0)
 
     lane = lax.broadcasted_iota(jnp.int32, (128, 128), 1)
     subl = lax.broadcasted_iota(jnp.int32, (128, 128), 0)
@@ -245,7 +241,6 @@
     mrun[...] = jnp.full((8, 2 * QW), LOW, F32)
     lrun[...] = jnp.zeros((8, 2 * QW), F32)
 
-    relay(ksems, 1)
     local(4).wait()
     local(5).wait()
     lane16 = lax.broadcasted_iota(jnp.int32, (16, 128), 1)
@@ -290,13 +285,23 @@
                 merge(p3, m, mo, sl)
 
     def prompt_stats(i, carry):
-        @pl.when(i < NZ - 2)
+        @pl.when(i == 1)
         def _():
-            relay(ksems, i + 2)
-
-        @pl.when(i < NZ - 1)
+            relay(ksems, 2, 3)
+            relay(ksems, NZ - 2, NZ - 3)
+            begin(vsems, 0)
+            arrived(ksems, 1)
+            arrived(ksems, 2)
+
+        @pl.when(i == 3)
         def _():
-            relay(vsems, i + 1)
+            swap_wait(vsems)
+            begin(vsems, 1)
+
+        @pl.when(i == 5)
+        def _():
+            for n in range(5, NZ):
+                arrived(ksems, n)
 
         d = zoff(i)
         share_wait(ksems, d, 0)
@@ -345,6 +350,13 @@
         merge(p3, m, mo, sl)
 
     def resp_stats(i, carry):
+        @pl.when(i == 2)
+        def _():
+            relay(vsems, 2, 3)
+            relay(vsems, NZ - 2, NZ - 3)
+            arrived(vsems, 1)
+            arrived(vsems, 2)
+
         stats_chunk(i, QW, False)
         return carry
 
@@ -409,7 +421,7 @@
         return remote(ysb.at[j], yrb.at[j], gys.at[j], gyr.at[j], (ypart, r))
 
     def z_send(j):
-        d = zoff(NZ - 1 - j)
+        d = zoff((j + 1) % NZ)
         return remote(zsb.at[j], zrb.at[NZ - d], gzs.at[d], gzr.at[NZ - d], (zpeer(d), r))
 
     def after_core(j):
@@ -424,9 +436,15 @@
         z_send(j).start()
 
     def grads(j, carry):
-        i = NZ - 1 - j
+        i = (j + 1) % NZ
         d = zoff(i)
         zc = lax.rem(z + d, NZ)
+
+        @pl.when(j == 2)
+        def _():
+            for n in range(5, NZ):
+                arrived(vsems, n)
+
         share_wait(vsems, d, 0)
         share_wait(vsems, d, 1)
         vc_rows = vv[pl.ds(zc * 4, 4)].reshape(CK, HD)
@@ -441,21 +459,21 @@
             psc[:, sl] = p.astype(BF16)
             dssc[:, sl] = ds
             dqT[:, sl] += dot(kTc, ds)
+            if t == 1:
+                @pl.when(j >= 1)
+                def _():
+                    after_core(j - 1)
+
+                @pl.when(j >= 2)
+                def _():
+                    after_y(j - 2)
+
         dk = dot(dssc[...], qa[...])
         dv = dot(psc[...], doa[...])
         for b in range(4):
             gpart[j, b % 2, b // 2, 0] = dk[b * BLK:(b + 1) * BLK, :]
             gpart[j, b % 2, b // 2, 1] = dv[b * BLK:(b + 1) * BLK, :]
         core_send(j).start()
-
-        @pl.when(j >= 1)
-        def _():
-            after_core(j - 1)
-
-        @pl.when(j >= 2)
-        def _():
-            after_y(j - 2)
-
         return carry
 
     lax.fori_loop(0, NZ, grads, 0)
@@ -471,8 +489,8 @@
     lax.fori_loop(1, nresp, send_back_q, 0)
     local(15).start()
 
+    after_y(NZ - 2)
     after_core(NZ - 1)
-    after_y(NZ - 2)
     for h in range(GROUP):
         dqloc[:, h * HD:(h + 1) * HD] = (dqT[:, h * BLK:(h + 1) * BLK].T * SCALE).astype(BF16)
     local(12).start()

time: 76.3 us -> 78 us (1.022)
  the two profiles are of different devices: /device:TPU:1 before, /device:TPU:6 now
where the time goes in v6:
time: 78 us; the launch traced here: 77.9 us
  Pallas kernels  77.2 us (99%)
    pallas_call x1, Pallas kernels, body(): pl.pallas_call(functools.partial(kernel, nresp), out_shape=(shape(prompt_...  75.4 us
    pallas_call x1, Pallas kernels, body(): pl.pallas_call(settle, out_shape=tuple((shape(part.shape, part.dtype) for...  1.89 us

profile of v6, /device:TPU:6, one launch (start us, length us, event | category | flops | bytes accessed | tf_op | source)
XLA Modules:
  0.0 77.9 jit_solution(12084140857433930644)
XLA Ops:
  0.6 75.4 %attn_bwd.1 = (bf16[128,1024]{1,0:T(8,128)(2,1)}, bf16[128,128]{1,0:T(8,128)(2,1)}, bf16[128,128]{1,0:T(8,128)(2,1)}, bf16[16,8192]{1,0:T(8,128)(2,1)}, bf16[16,...) custom-call(s32[16]{0:T(128)} %len_ref.1, s32[16]{0:T(128)} %row_ref.1, s32[32]{0:T(128)} %bi_ref.1, bf16[128,1024]{1,0:T(8,128)(2,1)} %pq.1, ...), custom_call_target="tpu_custom_call" | custom-call | tf_op jit(solution)/shard_map/attn_bwd/pallas_call | solution.py:565
  76.0 1.9 %settle.1 = (bf16[128,1024]{1,0:T(8,128)(2,1)}, bf16[128,128]{1,0:T(8,128)(2,1)}, bf16[128,128]{1,0:T(8,128)(2,1)}, bf16[16,8192]{1,0:T(8,128)(2,1)}, bf16[16,10...) custom-call(bf16[128,1024]{1,0:T(8,128)(2,1)} %get-tuple-element.12.refs_0_, bf16[128,128]{1,0:T(8,128)(2,1)} %get-tuple-element.13.refs_1_, ...), custom_call_target="tpu_custom_call" | custom-call | tf_op jit(solution)/shard_map/settle/pallas_call | solution.py:633

commit v7 on v6

--- a/solution.py
+++ b/solution.py
@@ -298,18 +298,13 @@
             swap_wait(vsems)
             begin(vsems, 1)
 
-        @pl.when(i == 5)
-        def _():
-            for n in range(5, NZ):
-                arrived(ksems, n)
-
         d = zoff(i)
         share_wait(ksems, d, 0)
         share_wait(ksems, d, 1)
         stats_chunk(i, 0, True)
         return carry
 
-    lax.fori_loop(0, NZ, prompt_stats, 0)
+    lax.fori_loop(0, 5, prompt_stats, 0)
 
     local(6).wait()
     acc = jnp.zeros((BLK, 128), F32)
@@ -350,17 +345,29 @@
         merge(p3, m, mo, sl)
 
     def resp_stats(i, carry):
-        @pl.when(i == 2)
+        stats_chunk(i, QW, False)
+        return carry
+
+    lax.fori_loop(0, 5, resp_stats, 0)
+    for n in range(5, NZ):
+        arrived(ksems, n)
+
+    def late_stats(i, carry):
+        @pl.when(i == NZ - 1)
         def _():
             relay(vsems, 2, 3)
             relay(vsems, NZ - 2, NZ - 3)
             arrived(vsems, 1)
             arrived(vsems, 2)
 
+        d = zoff(i)
+        share_wait(ksems, d, 0)
+        share_wait(ksems, d, 1)
+        stats_chunk(i, 0, True)
         stats_chunk(i, QW, False)
         return carry
 
-    lax.fori_loop(0, NZ, resp_stats, 0)
+    lax.fori_loop(5, NZ, late_stats, 0)
 
     peak = jnp.max(mrun[...], axis=0, keepdims=True)
     total = jnp.sum(lrun[...] * jnp.exp2((mrun[...] - peak) * EXP_SCALE), axis=0, keepdims=True)
@@ -459,21 +466,21 @@
             psc[:, sl] = p.astype(BF16)
             dssc[:, sl] = ds
             dqT[:, sl] += dot(kTc, ds)
-            if t == 1:
-                @pl.when(j >= 1)
-                def _():
-                    after_core(j - 1)
-
-                @pl.when(j >= 2)
-                def _():
-                    after_y(j - 2)
-
         dk = dot(dssc[...], qa[...])
         dv = dot(psc[...], doa[...])
         for b in range(4):
             gpart[j, b % 2, b // 2, 0] = dk[b * BLK:(b + 1) * BLK, :]
             gpart[j, b % 2, b // 2, 1] = dv[b * BLK:(b + 1) * BLK, :]
         core_send(j).start()
+
+        @pl.when(j >= 1)
+        def _():
+            after_core(j - 1)
+
+        @pl.when(j >= 2)
+        def _():
+            after_y(j - 2)
+
         return carry
 
     lax.fori_loop(0, NZ, grads, 0)
@@ -489,8 +496,8 @@
     lax.fori_loop(1, nresp, send_back_q, 0)
     local(15).start()
 
+    after_core(NZ - 1)
     after_y(NZ - 2)
-    after_core(NZ - 1)
     for h in range(GROUP):
         dqloc[:, h * HD:(h + 1) * HD] = (dqT[:, h * BLK:(h + 1) * BLK].T * SCALE).astype(BF16)
     local(12).start()

time: 78 us -> 74.9 us (0.960)
  the two profiles are of different devices: /device:TPU:6 before, /device:TPU:22 now
where the time goes in v7:
time: 74.9 us; the launch traced here: 74.8 us
  Pallas kernels  74.2 us (99%)
    pallas_call x1, Pallas kernels, body(): pl.pallas_call(functools.partial(kernel, nresp), out_shape=(shape(prompt_...  72.3 us
    pallas_call x1, Pallas kernels, body(): pl.pallas_call(settle, out_shape=tuple((shape(part.shape, part.dtype) for...  1.89 us

profile of v7, /device:TPU:22, one launch (start us, length us, event | category | flops | bytes accessed | tf_op | source)
XLA Modules:
  0.0 74.8 jit_solution(4882734743739438463)
XLA Ops:
  0.6 72.3 %attn_bwd.1 = (bf16[128,1024]{1,0:T(8,128)(2,1)}, bf16[128,128]{1,0:T(8,128)(2,1)}, bf16[128,128]{1,0:T(8,128)(2,1)}, bf16[16,8192]{1,0:T(8,128)(2,1)}, bf16[16,...) custom-call(s32[16]{0:T(128)} %len_ref.1, s32[16]{0:T(128)} %row_ref.1, s32[32]{0:T(128)} %bi_ref.1, bf16[128,1024]{1,0:T(8,128)(2,1)} %pq.1, ...), custom_call_target="tpu_custom_call" | custom-call | tf_op jit(solution)/shard_map/attn_bwd/pallas_call | solution.py:572
  72.9 1.9 %settle.1 = (bf16[128,1024]{1,0:T(8,128)(2,1)}, bf16[128,128]{1,0:T(8,128)(2,1)}, bf16[128,128]{1,0:T(8,128)(2,1)}, bf16[16,8192]{1,0:T(8,128)(2,1)}, bf16[16,10...) custom-call(bf16[128,1024]{1,0:T(8,128)(2,1)} %get-tuple-element.12.refs_0_, bf16[128,128]{1,0:T(8,128)(2,1)} %get-tuple-element.13.refs_1_, ...), custom_call_target="tpu_custom_call" | custom-call | tf_op jit(solution)/shard_map/settle/pallas_call | solution.py:640

commit v8 on v7

--- a/solution.py
+++ b/solution.py
@@ -35,8 +35,7 @@
     kk, vv, lq, lout, ldo, tout, tdo, rq, rdo, rk, rv, rdel, dbuf,
     qa, doa, qT, doT, pt, own_pt, mh, mrun, lrun, delta, dqT, psc, dssc, bias,
     gpart, grecv, kept, ysb, yrb, zsb, zrb, dqrows, dkrows, dvrows, dqloc, dkvloc,
-    kzs, kzr, kys, kyr, kcs, kcr, vzs, vzr, vys, vyr, vcs, vcr,
-    as_, ar_, gcs, gcr, gys, gyr, gzs, gzr, bs_, br_, loc,
+    kx, kzr, kcr, vx, vzr, vcr, as_, ar_, gs, gcr, gyr, gzr, bs_, br_, loc,
 ):
     c = lax.axis_index("ctx")
     r = lax.axis_index("resp")
@@ -58,6 +57,12 @@
         return pltpu.make_async_remote_copy(
             src_ref=src, dst_ref=dst, send_sem=ss, recv_sem=rs, device_id=dev, device_id_type=MESH
         )
+
+    def got(part, sem):
+        remote(part, part, sem, sem, (cpart, r)).wait_recv()
+
+    def sent(part, sem):
+        remote(part, part, sem, sem, (cpart, r)).wait_send()
 
     def zoff(i):
         return jnp.where(i % 2 == 1, (i + 1) // 2, (NZ - i // 2) % NZ)
@@ -115,37 +120,35 @@
     lax.fori_loop(1, nresp, greet_r, 0)
     pl.semaphore_wait(barrier, (NZ - 1) + (nresp - 1) + 2)
 
-    ksems = (kk, kzs, kzr, kys, kyr, kcs, kcr)
-    vsems = (vv, vzs, vzr, vys, vyr, vcs, vcr)
+    ksems = (kk, kx, kzr, kcr)
+    vsems = (vv, vx, vzr, vcr)
 
     def swap(sems):
-        ref, zs, zr, ys, yr, cs, cr = sems
-        return remote(ref.at[c], ref.at[c], ys.at[0], yr.at[0], (ypart, r))
+        ref, x, zr, cr = sems
+        return remote(ref.at[c], ref.at[c], x.at[0], x.at[1], (ypart, r))
 
     def swap_wait(sems):
-        ref, zs, zr, ys, yr, cs, cr = sems
-        remote(ref.at[ypart], ref.at[ypart], ys.at[0], yr.at[0], (ypart, r)).wait_recv()
+        ref, x, zr, cr = sems
+        got(ref.at[ypart], x.at[1])
 
     def hop(sems, d, e, far):
-        ref, zs, zr, ys, yr, cs, cr = sems
+        ref, x, zr, cr = sems
         b = zpeer(d) + far * ystep
         to = (zpeer(lax.rem(d - e + NZ, NZ)), r)
-        return remote(ref.at[b], ref.at[b], zs.at[e, far], zr.at[e, far], to)
+        return remote(ref.at[b], ref.at[b], x.at[0], zr.at[e, far], to)
 
     def hop_wait(sems, d, far):
-        ref, zs, zr, ys, yr, cs, cr = sems
+        ref, x, zr, cr = sems
+        got(ref.at[zpeer(d) + far * ystep], zr.at[d, far])
+
+    def share(sems, d, far):
+        ref, x, zr, cr = sems
         b = zpeer(d) + far * ystep
-        remote(ref.at[b], ref.at[b], zs.at[d, far], zr.at[d, far], (zpeer(1), r)).wait_recv()
-
-    def share(sems, d, far):
-        ref, zs, zr, ys, yr, cs, cr = sems
-        b = zpeer(d) + far * ystep
-        return remote(ref.at[b], ref.at[b], cs.at[d, far], cr.at[d, far], (cpart, r))
-
-    def share_wait(sems, d, far):
-        ref, zs, zr, ys, yr, cs, cr = sems
-        b = zpeer(d) + 1 - 2 * core + far * ystep
-        remote(ref.at[b], ref.at[b], cs.at[d, far], cr.at[d, far], (cpart, r)).wait_recv()
+        return remote(ref.at[b], ref.at[b], x.at[0], cr.at[d], (cpart, r))
+
+    def share_wait(sems, d):
+        ref, x, zr, cr = sems
+        got(ref.at[pl.ds(lax.rem(z + d, NZ) * 4, 2)], cr.at[d])
 
     def begin(sems, far):
         for e in (1, NZ - 1, 2, NZ - 2):
@@ -167,19 +170,8 @@
             share(sems, d, far).start()
 
     def drain_gather(sems):
-        def drain_hops(e, carry):
-            for far in range(2):
-                hop(sems, 0, e, far).wait_send()
-            return carry
-
-        def drain_shares(d, carry):
-            for far in range(2):
-                share(sems, d, far).wait_send()
-            return carry
-
-        lax.fori_loop(1, NZ, drain_hops, 0)
-        lax.fori_loop(0, NZ, drain_shares, 0)
-        swap(sems).wait_send()
+        ref, x, zr, cr = sems
+        sent(ref.at[pl.ds(0, 4 * NZ - 1)], x.at[0])
 
     def sources(p):
         return (cols(sq, p, QW), cols(sdo, p, QW), cols(sk, p, HD), cols(sv, p, HD), dbuf.at[p])
@@ -190,15 +182,8 @@
         p = rpeer(d)
         src = sources(p)
         return [
-            remote(src[n], slots(landings[n], r), as_.at[n, d], ar_.at[n, nresp - d], (c, p))
+            remote(src[n], slots(landings[n], r), as_.at[n], ar_.at[n], (c, p))
             for n in which
-        ]
-
-    def exchange_in(d):
-        p = rpeer(d)
-        return [
-            remote(slots(landings[n], p), slots(landings[n], p), as_.at[n, d], ar_.at[n, d], (c, p))
-            for n in range(5)
         ]
 
     def send_rows(n, carry):
@@ -299,8 +284,7 @@
             begin(vsems, 1)
 
         d = zoff(i)
-        share_wait(ksems, d, 0)
-        share_wait(ksems, d, 1)
+        share_wait(ksems, d)
         stats_chunk(i, 0, True)
         return carry
 
@@ -314,12 +298,9 @@
         acc = jnp.where(lane == h, jnp.sum(prod, axis=1, keepdims=True), acc)
     place_delta(acc, 0)
 
-    def wait_in(d, carry):
-        for cp in exchange_in(d):
-            cp.wait_recv()
-        return carry
-
-    lax.fori_loop(1, nresp, wait_in, 0)
+    others = 16 * (nresp - 1)
+    for n in range(5):
+        got(landings[n].at[pl.ds(0, others), :], ar_.at[n])
     for n in range(7, 12):
         local(n).wait()
     load_queries(rq, rdo, QW)
@@ -361,8 +342,7 @@
             arrived(vsems, 2)
 
         d = zoff(i)
-        share_wait(ksems, d, 0)
-        share_wait(ksems, d, 1)
+        share_wait(ksems, d)
         stats_chunk(i, 0, True)
         stats_chunk(i, QW, False)
         return carry
@@ -381,22 +361,12 @@
     def back(d, which):
         p = rpeer(d)
         dev = (c, p)
-        e = nresp - d
         out = (
-            lambda: remote(slots(dqrows, p), cols(dqr, r, QW), bs_.at[0, d], br_.at[0, e], dev),
-            lambda: remote(slots(dkrows, p), cols(dkr, r, HD), bs_.at[1, d], br_.at[1, e], dev),
-            lambda: remote(slots(dvrows, p), cols(dvr, r, HD), bs_.at[2, d], br_.at[2, e], dev),
+            lambda: remote(slots(dqrows, p), cols(dqr, r, QW), bs_.at[0], br_.at[0], dev),
+            lambda: remote(slots(dkrows, p), cols(dkr, r, HD), bs_.at[1], br_.at[1], dev),
+            lambda: remote(slots(dvrows, p), cols(dvr, r, HD), bs_.at[2], br_.at[2], dev),
         )
         return [out[n]() for n in which]
-
-    def back_in(d):
-        p = rpeer(d)
-        dev = (c, p)
-        return [
-            remote(cols(dqr, p, QW), cols(dqr, p, QW), bs_.at[0, d], br_.at[0, d], dev),
-            remote(cols(dkr, p, HD), cols(dkr, p, HD), bs_.at[1, d], br_.at[1, d], dev),
-            remote(cols(dvr, p, HD), cols(dvr, p, HD), bs_.at[2, d], br_.at[2, d], dev),
-        ]
 
     rkT = rk[...].T
     for h in range(GROUP):
@@ -422,14 +392,14 @@
     local(17).start()
 
     def core_send(j):
-        return remote(gpart.at[j, 1 - core], grecv.at[j], gcs.at[j], gcr.at[j], (cpart, r))
+        return remote(gpart.at[j, 1 - core], grecv.at[j], gs.at[0], gcr.at[j], (cpart, r))
 
     def y_send(j):
-        return remote(ysb.at[j], yrb.at[j], gys.at[j], gyr.at[j], (ypart, r))
+        return remote(ysb.at[j], yrb.at[j], gs.at[1], gyr.at[j], (ypart, r))
 
     def z_send(j):
         d = zoff((j + 1) % NZ)
-        return remote(zsb.at[j], zrb.at[NZ - d], gzs.at[d], gzr.at[NZ - d], (zpeer(d), r))
+        return remote(zsb.at[j], zrb.at[NZ - d], gs.at[2], gzr.at[0], (zpeer(d), r))
 
     def after_core(j):
         core_send(j).wait_recv()
@@ -452,8 +422,7 @@
             for n in range(5, NZ):
                 arrived(vsems, n)
 
-        share_wait(vsems, d, 0)
-        share_wait(vsems, d, 1)
+        share_wait(vsems, d)
         vc_rows = vv[pl.ds(zc * 4, 4)].reshape(CK, HD)
         kTc = kk[pl.ds(zc * 4, 4)].reshape(CK, HD).T
         prow = pl.ds(pl.multiple_of(i * CK, CK), CK)
@@ -504,47 +473,24 @@
     y_send(NZ - 1).wait_recv()
     kept[NZ - 1] = kept[NZ - 1] + yrb[NZ - 1].astype(F32)
 
+    got(zrb.at[pl.ds(0, NZ - 1)], gzr.at[0])
+    total_kv = kept[NZ - 1]
+    for n in range(1, NZ):
+        total_kv = total_kv + zrb[n].astype(F32)
+    dkvloc[0] = (total_kv[0] * SCALE).astype(BF16)
+    dkvloc[1] = total_kv[1].astype(BF16)
+    local(13).start()
+    local(14).start()
     drain_gather(ksems)
     drain_gather(vsems)
-
-    def drain_exchange(d, carry):
-        for cp in exchange(d, range(5)):
-            cp.wait_send()
-        return carry
-
-    lax.fori_loop(1, nresp, drain_exchange, 0)
-
-    def drain_parts(j, carry):
-        core_send(j).wait_send()
-        y_send(j).wait_send()
-        return carry
-
-    lax.fori_loop(0, NZ, drain_parts, 0)
-
-    def drain_zparts(j, carry):
-        z_send(j).wait_send()
-        return carry
-
-    def z_parts(d, carry):
-        remote(zrb.at[d], zrb.at[d], gzs.at[d], gzr.at[d], (zpeer(d), r)).wait_recv()
-        kept[NZ - 1] = kept[NZ - 1] + zrb[d].astype(F32)
-        return carry
-
-    lax.fori_loop(1, NZ, z_parts, 0)
-    dkvloc[0] = (kept[NZ - 1, 0] * SCALE).astype(BF16)
-    dkvloc[1] = kept[NZ - 1, 1].astype(BF16)
-    local(13).start()
-    local(14).start()
-    lax.fori_loop(0, NZ - 1, drain_zparts, 0)
-
-    def finish_back(d, carry):
-        for cp in back(d, range(3)):
-            cp.wait_send()
-        for cp in back_in(d):
-            cp.wait_recv()
-        return carry
-
-    lax.fori_loop(1, nresp, finish_back, 0)
+    for n in range(5):
+        sent(landings[n].at[pl.ds(0, others), :], as_.at[n])
+    sent(grecv, gs.at[0])
+    sent(ysb, gs.at[1])
+    sent(zsb.at[pl.ds(0, NZ - 1)], gs.at[2])
+    for n, (rows, part) in enumerate(((dqrows, dqr), (dkrows, dkr), (dvrows, dvr))):
+        sent(rows.at[pl.ds(0, others), :], bs_.at[n])
+        got(part.at[:, pl.ds(0, part.shape[1] * (nresp - 1) // nresp)], br_.at[n])
     for n in range(12, 18):
         local(n).wait()
 
@@ -621,11 +567,11 @@
                 pltpu.VMEM((BLK, HD), BF16),
                 pltpu.VMEM((BLK, QW), BF16),
                 pltpu.VMEM((2, BLK, HD), BF16),
-                dma((NZ, 2)), dma((NZ, 2)), dma((1,)), dma((1,)), dma((NZ, 2)), dma((NZ, 2)),
-                dma((NZ, 2)), dma((NZ, 2)), dma((1,)), dma((1,)), dma((NZ, 2)), dma((NZ, 2)),
-                dma((5, nresp)), dma((5, nresp)),
-                dma((NZ,)), dma((NZ,)), dma((NZ,)), dma((NZ,)), dma((NZ,)), dma((NZ,)),
-                dma((3, nresp)), dma((3, nresp)),
+                dma((2,)), dma((NZ, 2)), dma((NZ,)),
+                dma((2,)), dma((NZ, 2)), dma((NZ,)),
+                dma((5,)), dma((5,)),
+                dma((3,)), dma((NZ,)), dma((NZ,)), dma((1,)),
+                dma((3,)), dma((3,)),
                 dma((18,)),
             ],
             compiler_params=pltpu.CompilerParams(

time: 74.9 us -> 72.9 us (0.973)
  Pallas kernels: 74.2 us -> 72.1 us
    pallas_call x1, Pallas kernels: 72.3 us -> 70.2 us  [body(): pl.pallas_call(functools.partial(kernel, nresp), out_shape=(shape(prompt_...]
where the time goes in v8:
time: 72.9 us; the launch traced here: 72.8 us
  Pallas kernels  72.1 us (99%)
    pallas_call x1, Pallas kernels, body(): pl.pallas_call(functools.partial(kernel, nresp), out_shape=(shape(prompt_...  70.2 us
    pallas_call x1, Pallas kernels, body(): pl.pallas_call(settle, out_shape=tuple((shape(part.shape, part.dtype) for...  1.89 us

profile of v8, /device:TPU:22, one launch (start us, length us, event | category | flops | bytes accessed | tf_op | source)
XLA Modules:
  0.0 72.8 jit_solution(1315957453293538891)
XLA Ops:
  0.6 70.2 %attn_bwd.1 = (bf16[128,1024]{1,0:T(8,128)(2,1)}, bf16[128,128]{1,0:T(8,128)(2,1)}, bf16[128,128]{1,0:T(8,128)(2,1)}, bf16[16,8192]{1,0:T(8,128)(2,1)}, bf16[16,...) custom-call(s32[16]{0:T(128)} %len_ref.1, s32[16]{0:T(128)} %row_ref.1, s32[32]{0:T(128)} %bi_ref.1, bf16[128,1024]{1,0:T(8,128)(2,1)} %pq.1, ...), custom_call_target="tpu_custom_call" | custom-call | tf_op jit(solution)/shard_map/attn_bwd/pallas_call | solution.py:518
  70.9 1.9 %settle.1 = (bf16[128,1024]{1,0:T(8,128)(2,1)}, bf16[128,128]{1,0:T(8,128)(2,1)}, bf16[128,128]{1,0:T(8,128)(2,1)}, bf16[16,8192]{1,0:T(8,128)(2,1)}, bf16[16,10...) custom-call(bf16[128,1024]{1,0:T(8,128)(2,1)} %get-tuple-element.12.refs_0_, bf16[128,128]{1,0:T(8,128)(2,1)} %get-tuple-element.13.refs_1_, ...), custom_call_target="tpu_custom_call" | custom-call | tf_op jit(solution)/shard_map/settle/pallas_call | solution.py:586

commit v9 on v8

--- a/solution.py
+++ b/solution.py
@@ -16,6 +16,7 @@
 QW = GROUP * BLK
 CK = 4 * BLK
 QT = 512
+GT = 1024
 SCALE = HD ** -0.5
 EXP_SCALE = SCALE * 1.4426950408889634
 LOW = -1e30
@@ -29,9 +30,10 @@
 
 def kernel(
     nresp,
-    len_ref, row_ref, bi_ref,
+    len_any, row_any, bi_any,
     pq, pk, pv, pout, pdo, sq, sk, sv, sout, sdo,
     dqp, dkp, dvp, dqr, dkr, dvr,
+    len_ref, row_ref, bi_ref,
     kk, vv, lq, lout, ldo, tout, tdo, rq, rdo, rk, rv, rdel, dbuf,
     qa, doa, qT, doT, pt, own_pt, mh, mrun, lrun, delta, dqT, psc, dssc, bias,
     gpart, grecv, kept, ysb, yrb, zsb, zrb, dqrows, dkrows, dvrows, dqloc, dkvloc,
@@ -92,13 +94,16 @@
         lambda: (slots(dqrows, r), cols(dqr, r, QW)),
         lambda: (slots(dkrows, r), cols(dkr, r, HD)),
         lambda: (slots(dvrows, r), cols(dvr, r, HD)),
+        lambda: (len_any, len_ref),
+        lambda: (row_any, row_ref),
+        lambda: (bi_any, bi_ref),
     )
 
     def local(n):
         src, dst = pairs[n]()
         return pltpu.make_async_copy(src, dst, loc.at[n])
 
-    for n in range(11):
+    for n in (*range(11), 18, 19, 20):
         local(n).start()
 
     barrier = pltpu.get_barrier_semaphore()
@@ -203,6 +208,8 @@
     lane = lax.broadcasted_iota(jnp.int32, (128, 128), 1)
     subl = lax.broadcasted_iota(jnp.int32, (128, 128), 0)
     diff = lane - subl
+    for n in (18, 19, 20):
+        local(n).wait()
     my = bi_ref[c]
 
     def load_queries(q, do, base):
@@ -426,11 +433,11 @@
         vc_rows = vv[pl.ds(zc * 4, 4)].reshape(CK, HD)
         kTc = kk[pl.ds(zc * 4, 4)].reshape(CK, HD).T
         prow = pl.ds(pl.multiple_of(i * CK, CK), CK)
-        for t in range(2 * QW // QT):
-            sl = slice(t * QT, (t + 1) * QT)
+        for t in range(2 * QW // GT):
+            sl = slice(t * GT, (t + 1) * GT)
             dp = dot(vc_rows, doT[:, sl])
             f = mh[pl.ds(i * 4, 4), :, sl][:, None]
-            p = (pt[prow, sl].astype(F32).reshape(4, BLK // 8, 8, QT) * f).reshape(CK, QT)
+            p = (pt[prow, sl].astype(F32).reshape(4, BLK // 8, 8, GT) * f).reshape(CK, GT)
             ds = (p * (dp - delta[:, sl])).astype(BF16)
             psc[:, sl] = p.astype(BF16)
             dssc[:, sl] = ds
@@ -511,7 +518,6 @@
         lengths, resp_row, block_index,
     ):
         shape = jax.ShapeDtypeStruct
-        smem = pl.BlockSpec(memory_space=pltpu.SMEM)
         vmem = pl.BlockSpec(memory_space=pltpu.VMEM)
         dma = pltpu.SemaphoreType.DMA
         anywhere = pl.BlockSpec(memory_space=pl.ANY)
@@ -525,9 +531,12 @@
                 shape(resp_k.shape, BF16),
                 shape(resp_v.shape, BF16),
             ),
-            in_specs=[smem] * 3 + [anywhere] * 10,
+            in_specs=[anywhere] * 13,
             out_specs=(anywhere,) * 6,
             scratch_shapes=[
+                pltpu.SMEM(lengths.shape, jnp.int32),
+                pltpu.SMEM(resp_row.shape, jnp.int32),
+                pltpu.SMEM(block_index.shape, jnp.int32),
                 pltpu.VMEM((nctx, BLK, HD), BF16),
                 pltpu.VMEM((nctx, BLK, HD), BF16),
                 pltpu.VMEM((BLK, QW), BF16),
@@ -572,7 +581,7 @@
                 dma((5,)), dma((5,)),
                 dma((3,)), dma((NZ,)), dma((NZ,)), dma((1,)),
                 dma((3,)), dma((3,)),
-                dma((18,)),
+                dma((21,)),
             ],
             compiler_params=pltpu.CompilerParams(
                 collective_id=0, has_side_effects=True, vmem_limit_bytes=60 * 1024 * 1024

time: 72.9 us -> 71 us (0.974)
  Pallas kernels: 72.1 us -> 70.3 us
    pallas_call x1, Pallas kernels: 70.2 us -> 68.4 us  [body(): pl.pallas_call(functools.partial(kernel, nresp), out_shape=(shape(prompt_...]
where the time goes in v9:
time: 71 us; the launch traced here: 70.9 us
  Pallas kernels  70.3 us (99%)
    pallas_call x1, Pallas kernels, body(): pl.pallas_call(functools.partial(kernel, nresp), out_shape=(shape(prompt_...  68.4 us
    pallas_call x1, Pallas kernels, body(): pl.pallas_call(settle, out_shape=tuple((shape(part.shape, part.dtype) for...  1.89 us

profile of v9, /device:TPU:22, one launch (start us, length us, event | category | flops | bytes accessed | tf_op | source)
XLA Modules:
  0.0 70.9 jit_solution(11350362515045174039)
XLA Ops:
  0.6 68.4 %attn_bwd.1 = (bf16[128,1024]{1,0:T(8,128)(2,1)}, bf16[128,128]{1,0:T(8,128)(2,1)}, bf16[128,128]{1,0:T(8,128)(2,1)}, bf16[16,8192]{1,0:T(8,128)(2,1)}, bf16[16,...) custom-call(s32[16]{0:T(128)} %len_any.1, s32[16]{0:T(128)} %row_any.1, s32[32]{0:T(128)} %bi_any.1, bf16[128,1024]{1,0:T(8,128)(2,1)} %pq.1, ...), custom_call_target="tpu_custom_call" | custom-call | tf_op jit(solution)/shard_map/attn_bwd/pallas_call | solution.py:524
  69.0 1.9 %settle.1 = (bf16[128,1024]{1,0:T(8,128)(2,1)}, bf16[128,128]{1,0:T(8,128)(2,1)}, bf16[128,128]{1,0:T(8,128)(2,1)}, bf16[16,8192]{1,0:T(8,128)(2,1)}, bf16[16,10...) custom-call(bf16[128,1024]{1,0:T(8,128)(2,1)} %get-tuple-element.12.refs_0_, bf16[128,128]{1,0:T(8,128)(2,1)} %get-tuple-element.13.refs_1_, ...), custom_call_target="tpu_custom_call" | custom-call | tf_op jit(solution)/shard_map/settle/pallas_call | solution.py:595

commit v10 on v9

--- a/solution.py
+++ b/solution.py
@@ -68,6 +68,9 @@
 
     def zoff(i):
         return jnp.where(i % 2 == 1, (i + 1) // 2, (NZ - i // 2) % NZ)
+
+    def order(j):
+        return jnp.where(j < 2, j + 1, jnp.where(j < 5, j + 3, jnp.where(j < 7, j - 2, 0)))
 
     def cols(ref, p, w):
         return ref.at[:, pl.ds(pl.multiple_of(p * w, 128), w)]
@@ -405,7 +408,7 @@
         return remote(ysb.at[j], yrb.at[j], gs.at[1], gyr.at[j], (ypart, r))
 
     def z_send(j):
-        d = zoff((j + 1) % NZ)
+        d = zoff(order(j))
         return remote(zsb.at[j], zrb.at[NZ - d], gs.at[2], gzr.at[0], (zpeer(d), r))
 
     def after_core(j):
@@ -419,15 +422,16 @@
         zsb[j] = (kept[j] + yrb[j].astype(F32)).astype(BF16)
         z_send(j).start()
 
-    def grads(j, carry):
-        i = (j + 1) % NZ
+    def grads(j, last):
+        i = order(j)
         d = zoff(i)
         zc = lax.rem(z + d, NZ)
 
-        @pl.when(j == 2)
-        def _():
-            for n in range(5, NZ):
-                arrived(vsems, n)
+        if not last:
+            @pl.when(j == 1)
+            def _():
+                for n in range(5, NZ):
+                    arrived(vsems, n)
 
         share_wait(vsems, d)
         vc_rows = vv[pl.ds(zc * 4, 4)].reshape(CK, HD)
@@ -442,12 +446,17 @@
             psc[:, sl] = p.astype(BF16)
             dssc[:, sl] = ds
             dqT[:, sl] += dot(kTc, ds)
+        if last:
+            after_core(j - 1)
         dk = dot(dssc[...], qa[...])
         dv = dot(psc[...], doa[...])
         for b in range(4):
             gpart[j, b % 2, b // 2, 0] = dk[b * BLK:(b + 1) * BLK, :]
             gpart[j, b % 2, b // 2, 1] = dv[b * BLK:(b + 1) * BLK, :]
         core_send(j).start()
+        if last:
+            after_y(j - 2)
+            return
 
         @pl.when(j >= 1)
         def _():
@@ -457,9 +466,12 @@
         def _():
             after_y(j - 2)
 
-        return carry
-
-    lax.fori_loop(0, NZ, grads, 0)
+    def grads_step(j, carry):
+        grads(j, False)
+        return carry
+
+    lax.fori_loop(0, NZ - 1, grads_step, 0)
+    grads(NZ - 1, True)
 
     for h in range(GROUP):
         dqrows[:, h * HD:(h + 1) * HD] = (dqT[:, QW + h * BLK:QW + (h + 1) * BLK].T * SCALE).astype(BF16)

time: 71 us -> 69 us (0.972)
  the two profiles are of different devices: /device:TPU:22 before, /device:TPU:1 now
where the time goes in v10:
time: 69 us; the launch traced here: 67.7 us
  Pallas kernels  67 us (97%)
    pallas_call x1, Pallas kernels, body(): pl.pallas_call(functools.partial(kernel, nresp), out_shape=(shape(prompt_...  65.1 us
    pallas_call x1, Pallas kernels, body(): pl.pallas_call(settle, out_shape=tuple((shape(part.shape, part.dtype) for...  1.89 us

profile of v10, /device:TPU:1, one launch (start us, length us, event | category | flops | bytes accessed | tf_op | source)
XLA Modules:
  0.0 67.7 jit_solution(9546265036932203837)
XLA Ops:
  0.6 65.1 %attn_bwd.1 = (bf16[128,1024]{1,0:T(8,128)(2,1)}, bf16[128,128]{1,0:T(8,128)(2,1)}, bf16[128,128]{1,0:T(8,128)(2,1)}, bf16[16,8192]{1,0:T(8,128)(2,1)}, bf16[16,...) custom-call(s32[16]{0:T(128)} %len_any.1, s32[16]{0:T(128)} %row_any.1, s32[32]{0:T(128)} %bi_any.1, bf16[128,1024]{1,0:T(8,128)(2,1)} %pq.1, ...), custom_call_target="tpu_custom_call" | custom-call | tf_op jit(solution)/shard_map/attn_bwd/pallas_call | solution.py:536
  65.8 1.9 %settle.1 = (bf16[128,1024]{1,0:T(8,128)(2,1)}, bf16[128,128]{1,0:T(8,128)(2,1)}, bf16[128,128]{1,0:T(8,128)(2,1)}, bf16[16,8192]{1,0:T(8,128)(2,1)}, bf16[16,10...) custom-call(bf16[128,1024]{1,0:T(8,128)(2,1)} %get-tuple-element.12.refs_0_, bf16[128,128]{1,0:T(8,128)(2,1)} %get-tuple-element.13.refs_1_, ...), custom_call_target="tpu_custom_call" | custom-call | tf_op jit(solution)/shard_map/settle/pallas_call | solution.py:607

commit v11 on v10

--- a/solution.py
+++ b/solution.py
@@ -70,7 +70,7 @@
         return jnp.where(i % 2 == 1, (i + 1) // 2, (NZ - i // 2) % NZ)
 
     def order(j):
-        return jnp.where(j < 2, j + 1, jnp.where(j < 5, j + 3, jnp.where(j < 7, j - 2, 0)))
+        return jnp.where(j < 3, j + 1, jnp.where(j < 6, j + 2, jnp.where(j < 7, 4, 0)))
 
     def cols(ref, p, w):
         return ref.at[:, pl.ds(pl.multiple_of(p * w, 128), w)]
@@ -204,9 +204,9 @@
     begin(ksems, 0)
     local(1).wait()
     swap(vsems).start()
-    lax.fori_loop(1, nresp, send_rows, 0)
     swap_wait(ksems)
     begin(ksems, 1)
+    lax.fori_loop(1, nresp, send_rows, 0)
 
     lane = lax.broadcasted_iota(jnp.int32, (128, 128), 1)
     subl = lax.broadcasted_iota(jnp.int32, (128, 128), 0)
@@ -342,12 +342,12 @@
     lax.fori_loop(0, 5, resp_stats, 0)
     for n in range(5, NZ):
         arrived(ksems, n)
+    relay(vsems, 2, 3)
+    relay(vsems, NZ - 2, NZ - 3)
 
     def late_stats(i, carry):
         @pl.when(i == NZ - 1)
         def _():
-            relay(vsems, 2, 3)
-            relay(vsems, NZ - 2, NZ - 3)
             arrived(vsems, 1)
             arrived(vsems, 2)
 
@@ -428,7 +428,7 @@
         zc = lax.rem(z + d, NZ)
 
         if not last:
-            @pl.when(j == 1)
+            @pl.when(j == 2)
             def _():
                 for n in range(5, NZ):
                     arrived(vsems, n)

time: 69 us -> 69.5 us (level); the launches traced: 67.7 us -> 69.4 us
  Pallas kernels: 67 us -> 68.7 us
    pallas_call x1, Pallas kernels: 65.1 us -> 66.8 us  [body(): pl.pallas_call(functools.partial(kernel, nresp), out_shape=(shape(prompt_...]
where the time goes in v11:
time: 69.5 us; the launch traced here: 69.4 us
  Pallas kernels  68.7 us (99%)
    pallas_call x1, Pallas kernels, body(): pl.pallas_call(functools.partial(kernel, nresp), out_shape=(shape(prompt_...  66.8 us
    pallas_call x1, Pallas kernels, body(): pl.pallas_call(settle, out_shape=tuple((shape(part.shape, part.dtype) for...  1.89 us

profile of v11, /device:TPU:1, one launch (start us, length us, event | category | flops | bytes accessed | tf_op | source)
XLA Modules:
  0.0 69.4 jit_solution(3086025364625721874)
XLA Ops:
  0.6 66.8 %attn_bwd.1 = (bf16[128,1024]{1,0:T(8,128)(2,1)}, bf16[128,128]{1,0:T(8,128)(2,1)}, bf16[128,128]{1,0:T(8,128)(2,1)}, bf16[16,8192]{1,0:T(8,128)(2,1)}, bf16[16,...) custom-call(s32[16]{0:T(128)} %len_any.1, s32[16]{0:T(128)} %row_any.1, s32[32]{0:T(128)} %bi_any.1, bf16[128,1024]{1,0:T(8,128)(2,1)} %pq.1, ...), custom_call_target="tpu_custom_call" | custom-call | tf_op jit(solution)/shard_map/attn_bwd/pallas_call | solution.py:536
  67.5 1.9 %settle.1 = (bf16[128,1024]{1,0:T(8,128)(2,1)}, bf16[128,128]{1,0:T(8,128)(2,1)}, bf16[128,128]{1,0:T(8,128)(2,1)}, bf16[16,8192]{1,0:T(8,128)(2,1)}, bf16[16,10...) custom-call(bf16[128,1024]{1,0:T(8,128)(2,1)} %get-tuple-element.12.refs_0_, bf16[128,128]{1,0:T(8,128)(2,1)} %get-tuple-element.13.refs_1_, ...), custom_call_target="tpu_custom_call" | custom-call | tf_op jit(solution)/shard_map/settle/pallas_call | solution.py:607

commit v12 on v11

--- a/solution.py
+++ b/solution.py
@@ -448,6 +448,7 @@
             dqT[:, sl] += dot(kTc, ds)
         if last:
             after_core(j - 1)
+            after_y(j - 3)
         dk = dot(dssc[...], qa[...])
         dv = dot(psc[...], doa[...])
         for b in range(4):
@@ -462,9 +463,9 @@
         def _():
             after_core(j - 1)
 
-        @pl.when(j >= 2)
+        @pl.when(j >= 3)
         def _():
-            after_y(j - 2)
+            after_y(j - 3)
 
     def grads_step(j, carry):
         grads(j, False)

time: 69.5 us -> 68.5 us (0.986); the launches traced: 69.4 us -> 67.6 us
  Pallas kernels: 68.7 us -> 67 us
    pallas_call x1, Pallas kernels: 66.8 us -> 65.1 us  [body(): pl.pallas_call(functools.partial(kernel, nresp), out_shape=(shape(prompt_...]
where the time goes in v12:
time: 68.5 us; the launch traced here: 67.6 us
  Pallas kernels  67 us (98%)
    pallas_call x1, Pallas kernels, body(): pl.pallas_call(functools.partial(kernel, nresp), out_shape=(shape(prompt_...  65.1 us
    pallas_call x1, Pallas kernels, body(): pl.pallas_call(settle, out_shape=tuple((shape(part.shape, part.dtype) for...  1.89 us

profile of v12, /device:TPU:1, one launch (start us, length us, event | category | flops | bytes accessed | tf_op | source)
XLA Modules:
  0.0 67.6 jit_solution(11609008725611322987)
XLA Ops:
  0.6 65.1 %attn_bwd.1 = (bf16[128,1024]{1,0:T(8,128)(2,1)}, bf16[128,128]{1,0:T(8,128)(2,1)}, bf16[128,128]{1,0:T(8,128)(2,1)}, bf16[16,8192]{1,0:T(8,128)(2,1)}, bf16[16,...) custom-call(s32[16]{0:T(128)} %len_any.1, s32[16]{0:T(128)} %row_any.1, s32[32]{0:T(128)} %bi_any.1, bf16[128,1024]{1,0:T(8,128)(2,1)} %pq.1, ...), custom_call_target="tpu_custom_call" | custom-call | tf_op jit(solution)/shard_map/attn_bwd/pallas_call | solution.py:537
  65.7 1.9 %settle.1 = (bf16[128,1024]{1,0:T(8,128)(2,1)}, bf16[128,128]{1,0:T(8,128)(2,1)}, bf16[128,128]{1,0:T(8,128)(2,1)}, bf16[16,8192]{1,0:T(8,128)(2,1)}, bf16[16,10...) custom-call(bf16[128,1024]{1,0:T(8,128)(2,1)} %get-tuple-element.12.refs_0_, bf16[128,128]{1,0:T(8,128)(2,1)} %get-tuple-element.13.refs_1_, ...), custom_call_target="tpu_custom_call" | custom-call | tf_op jit(solution)/shard_map/settle/pallas_call | solution.py:608
